TPU v7x, 32 devices: a whole 2x2x4 slice. The times are simulated.
32 devices in a mesh: tm: 4 (over y, core), pix: 8 (over z, x).
Axes of the slice: x: 2, y: 2, z: 4, core: 2. Of those that a mesh axis runs over, the one named last changes fastest.
Arguments:
- activations: bfloat16 [4, 20480, 256], P('tm', 'pix'), may hold values from -6 to 6
- down_weight: bfloat16 [1024, 256], replicated, may hold values from -0.1875 to 0.1875
- down_bias: float32 [256], replicated, may hold values from -3 to 3
- taps: float32 [9, 256], replicated, may hold values from -2 to 2
- point_weight: bfloat16 [256, 256], replicated, may hold values from -0.375 to 0.375
- time_mix: float32 [4, 4, 256], replicated, may hold values from -3 to 3
- edge_rows: int32 [8, 2, 20], P('pix'), may hold values from 0 to 19, as said below
- cotangent: bfloat16 [4, 5120, 256], P(None, ('pix', 'tm')), may hold values from -6 to 6
Outputs:
- grad_input: bfloat16 [4, 20480, 256], P('tm', 'pix')
- grad_down: float32 [1024, 256], replicated
- grad_bias: float32 [256], replicated
- grad_taps: float32 [9, 256], replicated
- grad_point: float32 [256, 256], replicated
- grad_mix: float32 [4, 4, 256], replicated
Inputs may be any that keep to these rules, and one draw needn't show every extreme that they name: Each edge_rows[t, e] is either 0, 1, .., 19 or its reversal; edge_rows[t, 1] equals edge_rows[(t + 1) mod 8, 0].
All inputs are finite; a program needn't handle non-finite values.
Results may differ from a plain program's by a relative error of at most 0.014.
Values may be sent and summed in bfloat16 or wider, within the bound.
A program may use at most 64 MiB of HBM per device.

v0:
```python
import math

import jax
import jax.numpy as jnp
from jax import lax
from jax.sharding import PartitionSpec as P

C = 256
TR = 20
TC = 32


def padded_2(cells, sides, width):
    for axis, dim in sides:
        count = lax.axis_size(axis)
        head = lax.slice_in_dim(cells, 0, width, axis=dim)
        tail = lax.slice_in_dim(cells, cells.shape[dim] - width, cells.shape[dim], axis=dim)
        cells = jnp.concatenate(
            [
                lax.ppermute(tail, axis, [(i, (i + 1) % count) for i in range(count)]),
                cells,
                lax.ppermute(head, axis, [((i + 1) % count, i) for i in range(count)]),
            ],
            axis=dim,
        )
    return cells


def on_device(
    activations, down_weight, down_bias, taps, point_weight, time_mix, edge_rows, cotangent
):
    frames = lax.axis_size("tm")
    tiles = lax.axis_size("pix")
    pixels = TR * TC
    scale = 1.0 / math.sqrt(frames * tiles * pixels)
    rows_in = activations.reshape(pixels, 4 * C)
    preact = jnp.dot(rows_in, down_weight, preferred_element_type=jnp.float32) + down_bias
    pooled = jax.nn.silu(preact).astype(jnp.bfloat16)
    tile_grid = pooled.reshape(1, TR, TC, C)
    padded = padded_2(tile_grid, (("pix", 2),), 1)
    west_map = edge_rows[0, 0]
    east_map = edge_rows[0, 1]
    west_col = jnp.take(padded[0, :, 0, :], west_map, axis=0)
    east_col = jnp.take(padded[0, :, TC + 1, :], east_map, axis=0)
    widened = jnp.concatenate([west_col[:, None, :], tile_grid[0], east_col[:, None, :]], axis=1)
    widened = jnp.pad(widened, ((1, 1), (0, 0), (0, 0)))
    spread = jnp.zeros((TR, TC, C), jnp.float32)
    for row_off in range(3):
        for col_off in range(3):
            spread = (
                spread
                + taps[row_off * 3 + col_off]
                * widened[row_off : row_off + TR, col_off : col_off + TC, :]
            )
    spread_low = spread.astype(jnp.bfloat16).reshape(pixels, C)
    mixed_in = (
        pooled.astype(jnp.float32)
        + jnp.dot(spread_low, point_weight, preferred_element_type=jnp.float32)
    ).astype(jnp.bfloat16)
    by_pixel = lax.all_to_all(
        mixed_in.reshape(1, pixels, C), "tm", split_axis=1, concat_axis=0, tiled=True
    )
    mix_part = jnp.einsum("gpc,fpc->fgc", by_pixel, cotangent, preferred_element_type=jnp.float32)
    cot_f = cotangent.astype(jnp.float32)
    mixed_acc = jnp.zeros((frames, cotangent.shape[1], C), jnp.float32)
    for source in range(frames):
        mixed_acc = mixed_acc + time_mix[source][:, None, :] * cot_f[source][None, :, :]
    mixed_grad = mixed_acc.astype(jnp.bfloat16)
    back_grad = lax.all_to_all(mixed_grad, "tm", split_axis=0, concat_axis=1, tiled=True)
    mixed_rows = back_grad.reshape(pixels, C)
    point_part = jnp.dot(spread_low.T, mixed_rows, preferred_element_type=jnp.float32)
    spread_grad = jnp.dot(mixed_rows, point_weight.T, preferred_element_type=jnp.float32).astype(
        jnp.bfloat16
    )
    grad_float = spread_grad.reshape(TR, TC, C).astype(jnp.float32)
    taps_rows = []
    for row_off in range(3):
        for col_off in range(3):
            taps_rows.append(
                jnp.sum(
                    grad_float * widened[row_off : row_off + TR, col_off : col_off + TC, :],
                    axis=(0, 1),
                )
            )
    taps_part = jnp.stack(taps_rows, axis=0)
    grad_padded = jnp.pad(grad_float, ((2, 2), (2, 2), (0, 0)))
    wide_grad = jnp.zeros((TR + 2, TC + 2, C), jnp.float32)
    for row_off in range(3):
        for col_off in range(3):
            wide_grad = (
                wide_grad
                + taps[row_off * 3 + col_off]
                * grad_padded[2 - row_off : 4 - row_off + TR, 2 - col_off : 4 - col_off + TC, :]
            )
    west_back = jnp.take(wide_grad[1 : TR + 1, 0, :], west_map, axis=0)
    east_back = jnp.take(wide_grad[1 : TR + 1, TC + 1, :], east_map, axis=0)
    outgoing = jnp.stack([west_back, east_back], axis=1)
    incoming = padded_2(outgoing.astype(jnp.bfloat16), (("pix", 1),), 1).astype(outgoing.dtype)
    inner_grad = wide_grad[1 : TR + 1, 1 : TC + 1, :]
    inner_grad = inner_grad.at[:, 0, :].add(incoming[:, 0, :])
    inner_grad = inner_grad.at[:, TC - 1, :].add(incoming[:, 3, :])
    pooled_grad = mixed_rows.astype(jnp.float32) + inner_grad.reshape(pixels, C)
    sigma = jax.nn.sigmoid(preact)
    pre_grad = (pooled_grad * (sigma * (1.0 + preact * (1.0 - sigma)))).astype(jnp.bfloat16)
    bias_part = jnp.sum(pre_grad.astype(jnp.float32), axis=0)
    down_part = jnp.dot(rows_in.T, pre_grad, preferred_element_type=jnp.float32)
    grad_input = jnp.dot(pre_grad, down_weight.T, preferred_element_type=jnp.float32).astype(
        jnp.bfloat16
    )
    terms = (
        down_part,
        point_part,
        taps_part,
        mix_part.reshape(frames * frames, C),
        bias_part.reshape(1, C),
    )
    totals = lax.psum((terms[0], terms[1], terms[2], terms[3], terms[4]), ("tm", "pix"))
    grad_down = totals[0] * scale
    grad_point = totals[1] * scale
    grad_taps = totals[2] * scale
    grad_mix = totals[3].reshape(frames, frames, C) * scale
    grad_bias = totals[4].reshape(C) * scale
    return (
        grad_input.reshape(1, 4 * pixels, C),
        grad_down,
        grad_bias,
        grad_taps,
        grad_point,
        grad_mix,
    )


def solution(mesh):
    in_specs = (
        P("tm", "pix", None),
        P(),
        P(),
        P(),
        P(),
        P(),
        P("pix", None, None),
        P(None, ("pix", "tm"), None),
    )
    out_specs = (P("tm", "pix", None), P(), P(), P(), P(), P())
    return jax.shard_map(
        on_device, mesh=mesh, in_specs=in_specs, out_specs=out_specs, check_vma=False
    )
```

profile of v0, /device:TPU:0, one launch (start us, length us, event | category | flops | bytes accessed | tf_op | source)
XLA Modules:
  0.0 207.1 jit_solution(16027261836808091634)
XLA Ops:
  7.2 0.8 slice_bitcast_fusion.9
  8.0 1.0 convert_element_type.87
  9.1 0.9 add_convert_fusion
  10.0 4.2 %all-to-all-start = ((bf16[4,160,256]{2,1,0:T(8,128)(2,1)}), bf16[4,160,256]{2,1,0:T(8,128)(2,1)S(1)}, u32[]{:S(2)}, u32[]{:S(2)}) async-start(bf16[4,160,256]{2,1,0:T(8,128)(2,1)} %add_convert_fusion), calls=%async_computation | async-start | bytes 655360 | tf_op jit(solution)/shard_map/all_to_all | solution.py:69
  14.3 6.7 %all-to-all-done = bf16[4,160,256]{2,1,0:T(8,128)(2,1)S(1)} async-done(((bf16[4,160,256]{2,1,0:T(8,128)(2,1)}), bf16[4,160,256]{2,1,0:T(8,128)(2,1)S(1)}, u32[]{:S(2)}, u32[]{:S(2)}) %all-to-all-start) | async-done | bytes 327712 | tf_op jit(solution)/shard_map/all_to_all | solution.py:69
  22.2 0.9 copy-done.1
  23.8 5.2 %collective-permute-start.1 = (bf16[20,1,256]{2,0,1:T(8,128)(2,1)S(1)}, bf16[20,1,256]{2,0,1:T(8,128)(2,1)S(1)}, u32[]{:S(2)}, u32[]{:S(2)}) collective-permute-start(bf16[20,1,256]{2,0,1:T(8,128)(2,1)S(1)} %fusion.49), channel_id=1, source_target_pairs={{1,0},{2,1},{3,2},{4,3},{5,4},{6,5},{7,6},{0,7},{9,8},{10,9},{11,1... | collective-permute-start | bytes 30728 | tf_op jit(solution)/shard_map/ppermute | solution.py:22
  29.7 1.1 copy.60
  30.8 2.5 %reshape.139 = bf16[640,1024]{1,0:T(8,128)(2,1)S(1)} reshape(bf16[1,2560,256]{2,1,0:T(8,128)(2,1)} %param.16) | data formatting | bytes 2621440 | tf_op jit(solution)/shard_map/reshape | solution.py:36
  33.3 1.2 slice.257
  34.5 1.6 collective-permute-done
  37.8 1.6 convolution_bitcast_fusion
  39.4 3.2 %collective-permute-start.3 = (bf16[1,20,1,256]{3,1,2,0:T(8,128)(2,1)S(1)}, bf16[1,20,1,256]{3,1,2,0:T(8,128)(2,1)S(1)}, u32[]{:S(2)}, u32[]{:S(2)}) collective-permute-start(bf16[1,20,1,256]{3,1,2,0:T(8,128)(2,1)S(1)} %copy.65), channel_id=1, source_target_pairs={{1,0},{2,1},{3,2},{4,3},{5,4},{6,5},{7,6},{0,7},{9,8},{10,9},{11,1... | collective-permute-start | bytes 30728 | tf_op jit(solution)/shard_map/ppermute | solution.py:22
  43.2 1.6 reshape.140
  45.5 3.6 %collective-permute-done.2 = bf16[1,20,1,256]{3,1,2,0:T(8,128)(2,1)S(1)} collective-permute-done((bf16[1,20,1,256]{3,1,2,0:T(8,128)(2,1)S(1)}, bf16[1,20,1,256]{3,1,2,0:T(8,128)(2,1)S(1)}, u32[]{:S(2)}, u32[]{:S(2)}) %collective-permute-start.2) | collective-permute-done | bytes 10272 | tf_op jit(solution)/shard_map/ppermute | solution.py:20
  50.8 1.0 fusion.53
  53.0 2.7 %reduce.5 = bf16[640,256]{1,0:T(8,128)(2,1)S(1)} reduce(bf16[640,1,256]{2,1,0:T(2,128)(2,1)S(1)} %bitcast.105, bf16[]{:T(256)} %broadcast.135), dimensions={1}, to_apply=%bitcast.94.reduce_sub_computation | reduce | bytes 655362
  55.7 0.8 reshape.191
  56.5 3.5 %all-to-all-start.1 = ((bf16[4,2,20480]{2,1,0:T(2,128)(2,1)}), bf16[4,2,20480]{2,1,0:T(2,128)(2,1)S(1)}, u32[]{:S(2)}, u32[]{:S(2)}) async-start(bf16[4,2,20480]{2,1,0:T(2,128)(2,1)} %reshape.191), calls=%async_computation.1 | async-start | bytes 655360 | tf_op jit(solution)/shard_map/all_to_all | solution.py:60
  61.5 5.2 %all-to-all-done.1 = bf16[4,2,20480]{2,1,0:T(2,128)(2,1)S(1)} async-done(((bf16[4,2,20480]{2,1,0:T(2,128)(2,1)}), bf16[4,2,20480]{2,1,0:T(2,128)(2,1)S(1)}, u32[]{:S(2)}, u32[]{:S(2)}) %all-to-all-start.1) | async-done | bytes 327712 | tf_op jit(solution)/shard_map/all_to_all | solution.py:60
  68.1 37.6 %all-reduce.2 = (f32[1,256]{1,0:T(1,128)S(1)}, f32[9,256]{1,0:T(8,128)S(1)}, f32[16,256]{1,0:T(8,128)S(1)}) all-reduce(f32[1,256]{1,0:T(1,128)S(1)} %bitcast.136, f32[9,256]{1,0:T(8,128)S(1)} %stack.51, f32[16,256]{1,0:T(8,128)S(1)} %reshape.145), channel_id=1, replica_groups=mesh['tm'=4,'pix'=8] {'tm','pix'}, use_global_device_ids=true, to_apply=%region_2.4 | all-reduce | flops 6656 | bytes 53248 | tf_op jit(solution)/shard_map/psum | solution.py:117
  107.5 89.4 %all-reduce.6.cloned.1.call-done = (f32[1024,256]{0,1:T(8,128)}, f32[256,256]{1,0:T(8,128)}) async-done(((f32[1024,256]{0,1:T(8,128)}, f32[256,256]{1,0:T(8,128)}), (f32[1024,256]{0,1:T(8,128)}, f32[256,256]{1,0:T(8,128)})) %all-reduce.6.cloned.1.call-update) | async-done | bytes 1310736 | tf_op jit(solution)/shard_map/psum | solution.py:117
  196.9 1.3 broadcast_multiply_fusion
  198.2 1.3 copy.62
  (67 shorter events, 13.9 us)
Async XLA Ops:
  7.2 29.9 %copy-start = (bf16[1024,256]{1,0:T(8,128)(2,1)S(1)}, bf16[1024,256]{1,0:T(8,128)(2,1)}, u32[]{:S(2)}) copy-start(bf16[1024,256]{1,0:T(8,128)(2,1)} %param.17) | copy-start | bytes 1572868
  9.0 5.2 %copy-start.7 = (s32[1,2,20]{2,1,0:T(2,128)S(1)}, s32[1,2,20]{2,1,0:T(2,128)}, u32[]{:S(2)}) copy-start(s32[1,2,20]{2,1,0:T(2,128)} %param.22) | copy-start | bytes 484
  9.0 5.3 %copy-start.6 = (f32[9,256]{1,0:T(8,128)S(1)}, f32[9,256]{1,0:T(8,128)}, u32[]{:S(2)}) copy-start(f32[9,256]{1,0:T(8,128)} %param.19) | copy-start | bytes 27652
  9.0 11.9 %copy-start.3 = (bf16[256,256]{1,0:T(8,128)(2,1)S(1)}, bf16[256,256]{1,0:T(8,128)(2,1)}, u32[]{:S(2)}) copy-start(bf16[256,256]{1,0:T(8,128)(2,1)} %param.20) | copy-start | bytes 393220
  10.0 11.0 %all-to-all-start = ((bf16[4,160,256]{2,1,0:T(8,128)(2,1)}), bf16[4,160,256]{2,1,0:T(8,128)(2,1)S(1)}, u32[]{:S(2)}, u32[]{:S(2)}) async-start(bf16[4,160,256]{2,1,0:T(8,128)(2,1)} %add_convert_fusion), calls=%async_computation | async-start | bytes 655360 | tf_op jit(solution)/shard_map/all_to_all | solution.py:69
  21.6 8.0 %copy-start.2 = (bf16[4,160,256]{2,1,0:T(8,128)(2,1)S(1)}, bf16[4,160,256]{2,1,0:T(8,128)(2,1)}, u32[]{:S(2)}) copy-start(bf16[4,160,256]{2,1,0:T(8,128)(2,1)} %param.23) | copy-start | bytes 983044
  22.2 0.9 copy-start.1
  23.8 10.7 %collective-permute-start.1 = (bf16[20,1,256]{2,0,1:T(8,128)(2,1)S(1)}, bf16[20,1,256]{2,0,1:T(8,128)(2,1)S(1)}, u32[]{:S(2)}, u32[]{:S(2)}) collective-permute-start(bf16[20,1,256]{2,0,1:T(8,128)(2,1)S(1)} %fusion.49), channel_id=1, source_target_pairs={{1,0},{2,1},{3,2},{4,3},{5,4},{6,5},{7,6},{0,7},{9,8},{10,9},{11,1... | collective-permute-start | bytes 30728 | tf_op jit(solution)/shard_map/ppermute | solution.py:22
  29.7 6.4 %collective-permute-start = (bf16[20,1,256]{2,0,1:T(8,128)(2,1)S(1)}, bf16[20,1,256]{2,0,1:T(8,128)(2,1)S(1)}, u32[]{:S(2)}, u32[]{:S(2)}) collective-permute-start(bf16[20,1,256]{2,0,1:T(8,128)(2,1)S(1)} %fusion.48), channel_id=1, source_target_pairs={{0,1},{1,2},{2,3},{3,4},{4,5},{5,6},{6,7},{7,0},{8,9},{9,10},{10,1... | collective-permute-start | bytes 30728 | tf_op jit(solution)/shard_map/ppermute | solution.py:20
  33.3 3.8 %copy-start.8 = (f32[256]{0:T(256)S(1)}, f32[256]{0:T(256)}, u32[]{:S(2)}) copy-start(f32[256]{0:T(256)} %param.18) | copy-start | bytes 3076
  39.4 5.4 %collective-permute-start.3 = (bf16[1,20,1,256]{3,1,2,0:T(8,128)(2,1)S(1)}, bf16[1,20,1,256]{3,1,2,0:T(8,128)(2,1)S(1)}, u32[]{:S(2)}, u32[]{:S(2)}) collective-permute-start(bf16[1,20,1,256]{3,1,2,0:T(8,128)(2,1)S(1)} %copy.65), channel_id=1, source_target_pairs={{1,0},{2,1},{3,2},{4,3},{5,4},{6,5},{7,6},{0,7},{9,8},{10,9},{11,1... | collective-permute-start | bytes 30728 | tf_op jit(solution)/shard_map/ppermute | solution.py:22
  42.7 6.4 %collective-permute-start.2 = (bf16[1,20,1,256]{3,1,2,0:T(8,128)(2,1)S(1)}, bf16[1,20,1,256]{3,1,2,0:T(8,128)(2,1)S(1)}, u32[]{:S(2)}, u32[]{:S(2)}) collective-permute-start(bf16[1,20,1,256]{3,1,2,0:T(8,128)(2,1)S(1)} %copy.64), channel_id=1, source_target_pairs={{0,1},{1,2},{2,3},{3,4},{4,5},{5,6},{6,7},{7,0},{8,9},{9,10},{10,1... | collective-permute-start | bytes 30728 | tf_op jit(solution)/shard_map/ppermute | solution.py:20
  56.5 10.2 %all-to-all-start.1 = ((bf16[4,2,20480]{2,1,0:T(2,128)(2,1)}), bf16[4,2,20480]{2,1,0:T(2,128)(2,1)S(1)}, u32[]{:S(2)}, u32[]{:S(2)}) async-start(bf16[4,2,20480]{2,1,0:T(2,128)(2,1)} %reshape.191), calls=%async_computation.1 | async-start | bytes 655360 | tf_op jit(solution)/shard_map/all_to_all | solution.py:60
  60.0 136.9 %all-reduce.6.cloned.1.call-start = ((), (), s32[]{:S(2)}) async-start(), calls=%async_computation.2 | async-start | bytes 2621440 | tf_op jit(solution)/shard_map/psum | solution.py:117
  61.5 5.9 %copy-start.4 = (bf16[4,160,256]{1,0,2:T(4,128)(2,1)S(1)}, bf16[4,160,256]{1,0,2:T(4,128)(2,1)}, u32[]{:S(2)}) copy-start(bf16[4,160,256]{1,0,2:T(4,128)(2,1)} %copy.60) | copy-start | bytes 983044
  198.2 1.3 copy-start.5
Sparse Core Ops, SparseCore 0:
  66.8 130.0 all-reduce.5
where the time goes:
time: 208 us; the launch traced here: 207 us
  waiting for transfers between devices  107 us (51%)
  blocking collectives  37.6 us (18%)
  starting transfers between devices  16.1 us (8%)
  local copies, waits for them, and re-layouts  16 us (8%)
  between operations  14.4 us (7%)
  other arithmetic  11.1 us (5%)
  matrix products  4.8 us (2%)
    psum x1, waiting for transfers between devices, on_device(): lax.psum((terms[0], terms[1], terms[2], terms[3], terms[4]), ('tm', 'pix'))  89.4 us
    psum x1, blocking collectives, on_device(): lax.psum((terms[0], terms[1], terms[2], terms[3], terms[4]), ('tm', 'pix'))  37.6 us
    ppermute x2, starting transfers between devices, padded_2(): lax.ppermute(head, axis, [((i + 1) % count, i) for i in range(count)])  8.38 us
    all_to_all x1, waiting for transfers between devices, on_device(): lax.all_to_all(mixed_grad, 'tm', split_axis=0, concat_axis=1, tiled=True)  6.67 us
    all_to_all x1, waiting for transfers between devices, on_device(): lax.all_to_all(mixed_in.reshape(1, pixels, C), 'tm', split_axis=1, concat...  5.19 us
    ppermute x2, waiting for transfers between devices, padded_2(): lax.ppermute(tail, axis, [(i, (i + 1) % count) for i in range(count)])  5.16 us
    unnamed x26, local copies, waits for them, and re-layouts  5.03 us
    all_to_all x1, starting transfers between devices, on_device(): lax.all_to_all(mixed_grad, 'tm', split_axis=0, concat_axis=1, tiled=True)  4.24 us
  transfers between devices with their start and end apart: 7, of which 5 were waited for; matrix products, arithmetic and copies ran while one was open for 6% of the time, Pallas kernels for 0%

commit v1 on v0

--- a/solution.py
+++ b/solution.py
@@ -1,13 +1,17 @@
+import functools
 import math
 
 import jax
 import jax.numpy as jnp
 from jax import lax
+from jax.experimental import pallas as pl
+from jax.experimental.pallas import tpu as pltpu
 from jax.sharding import PartitionSpec as P
 
 C = 256
 TR = 20
 TC = 32
+MESH = pl.DeviceIdType.MESH
 
 
 def padded_2(cells, sides, width):
@@ -24,6 +28,146 @@
             axis=dim,
         )
     return cells
+
+
+def total_kernel(
+    rows, scale, down, point, taps, mix, bias, out_down, out_point, out_taps, out_mix, out_bias,
+    packed, core_in, half, parts, mine, gathered, other,
+    core_sems, part_send, part_recv, all_send, all_recv, pair_send, pair_recv,
+):
+    tm, pix = lax.axis_index("tm"), lax.axis_index("pix")
+    n_pix = lax.axis_size("pix")
+    group = lax.axis_size("tm") // 2 * n_pix
+    core = lax.rem(tm, 2)
+    me = tm // 2 * n_pix + pix
+    partner = (tm + 1 - 2 * core, pix)
+
+    def peer(step):
+        index = lax.rem(me + step, group)
+        return index, (index // n_pix * 2 + core, lax.rem(index, n_pix))
+
+    barrier = pltpu.get_barrier_semaphore()
+    pl.semaphore_signal(barrier, inc=1, device_id=partner, device_id_type=MESH)
+
+    @pl.loop(1, group)
+    def _(step):
+        _, device = peer(step)
+        pl.semaphore_signal(barrier, inc=1, device_id=device, device_id_type=MESH)
+
+    small = jnp.concatenate([taps[...], mix[...], bias[...], jnp.zeros((6, C), jnp.float32)], axis=0)
+    for side in range(2):
+        lanes = slice(side * 128, side * 128 + 128)
+        packed[side, 0:1024, :] = down[:, lanes].astype(jnp.bfloat16)
+        packed[side, 1024:1280, :] = point[:, lanes].astype(jnp.bfloat16)
+        packed[side, 1280:1312, :] = small[:, lanes].astype(jnp.bfloat16)
+        packed[side, 1312:, :] = jnp.zeros((group * rows - 1312, 128), jnp.bfloat16)
+    pl.semaphore_wait(barrier, group)
+
+    swap = pltpu.make_async_remote_copy(
+        packed.at[1 - core], core_in, core_sems.at[0], core_sems.at[1], partner, MESH
+    )
+    swap.start()
+    swap.wait()
+    half[...] = (packed[core].astype(jnp.float32) + core_in[...].astype(jnp.float32)).astype(
+        jnp.bfloat16
+    )
+
+    def block(ref, index):
+        return ref.at[pl.ds(pl.multiple_of(index * rows, 16), rows)]
+
+    def send_part(step):
+        index, device = peer(step)
+        return pltpu.make_async_remote_copy(
+            block(half, index), parts.at[step], part_send.at[step], part_recv.at[step], device, MESH
+        )
+
+    @pl.loop(1, group)
+    def _(step):
+        send_part(step).start()
+
+    parts[0] = half[pl.ds(pl.multiple_of(me * rows, 16), rows), :]
+
+    @pl.loop(1, group)
+    def _(step):
+        send_part(step).wait()
+
+    def add(step, total):
+        return total + parts[step].astype(jnp.float32)
+
+    mine[...] = lax.fori_loop(0, group, add, jnp.zeros((rows, 128), jnp.float32)).astype(
+        jnp.bfloat16
+    )
+
+    def send_all(step):
+        _, device = peer(step)
+        return pltpu.make_async_remote_copy(
+            mine, gathered.at[step], all_send.at[step], all_recv.at[step], device, MESH
+        )
+
+    def send_pair(step):
+        return pltpu.make_async_remote_copy(
+            gathered.at[step], other.at[step], pair_send.at[step], pair_recv.at[step], partner, MESH
+        )
+
+    @pl.loop(1, group)
+    def _(step):
+        send_all(step).start()
+
+    gathered[0] = mine[...]
+    send_pair(0).start()
+
+    @pl.loop(1, group)
+    def _(step):
+        send_all(step).wait()
+        send_pair(step).start()
+
+    @pl.loop(0, group)
+    def _(step):
+        send_pair(step).wait()
+
+    @pl.loop(0, group)
+    def _(step):
+        index = lax.rem(me + group - step, group)
+        place = pl.ds(pl.multiple_of(index * rows, 16), rows)
+        packed[core, place, :] = gathered[step]
+        packed[1 - core, place, :] = other[step]
+
+    for side in range(2):
+        lanes = slice(side * 128, side * 128 + 128)
+        out_down[:, lanes] = packed[side, 0:1024, :].astype(jnp.float32) * scale
+        out_point[:, lanes] = packed[side, 1024:1280, :].astype(jnp.float32) * scale
+        tail = packed[side, 1280:1312, :].astype(jnp.float32) * scale
+        out_taps[:, lanes] = tail[0:9]
+        out_mix[:, lanes] = tail[9:25]
+        out_bias[:, lanes] = tail[25:26]
+
+
+def total_over_devices(down, point, taps, mix, bias, scale):
+    group = lax.axis_size("tm") // 2 * lax.axis_size("pix")
+    rows = -(-1312 // (16 * group)) * 16
+    low = jnp.bfloat16
+    sems = pltpu.SemaphoreType.DMA((group,))
+    outs = [jax.ShapeDtypeStruct(x.shape, jnp.float32) for x in (down, point, taps, mix, bias)]
+    return pl.pallas_call(
+        functools.partial(total_kernel, rows, scale),
+        out_shape=outs,
+        in_specs=[pl.BlockSpec(memory_space=pltpu.VMEM)] * 5,
+        out_specs=[pl.BlockSpec(memory_space=pltpu.VMEM)] * 5,
+        scratch_shapes=[
+            pltpu.VMEM((2, group * rows, 128), low),
+            pltpu.VMEM((group * rows, 128), low),
+            pltpu.VMEM((group * rows, 128), low),
+            pltpu.VMEM((group, rows, 128), low),
+            pltpu.VMEM((rows, 128), low),
+            pltpu.VMEM((group, rows, 128), low),
+            pltpu.VMEM((group, rows, 128), low),
+            pltpu.SemaphoreType.DMA((2,)),
+            sems, sems, sems, sems, sems, sems,
+        ],
+        compiler_params=pltpu.CompilerParams(
+            collective_id=0, has_side_effects=True, vmem_limit_bytes=40 * 1024 * 1024
+        ),
+    )(down, point, taps, mix, bias)
 
 
 def on_device(
@@ -107,19 +251,17 @@
     grad_input = jnp.dot(pre_grad, down_weight.T, preferred_element_type=jnp.float32).astype(
         jnp.bfloat16
     )
-    terms = (
+    totals = total_over_devices(
         down_part,
         point_part,
         taps_part,
         mix_part.reshape(frames * frames, C),
         bias_part.reshape(1, C),
-    )
-    totals = lax.psum((terms[0], terms[1], terms[2], terms[3], terms[4]), ("tm", "pix"))
-    grad_down = totals[0] * scale
-    grad_point = totals[1] * scale
-    grad_taps = totals[2] * scale
-    grad_mix = totals[3].reshape(frames, frames, C) * scale
-    grad_bias = totals[4].reshape(C) * scale
+        scale,
+    )
+    grad_down, grad_point, grad_taps, grad_mix, grad_bias = totals
+    grad_mix = grad_mix.reshape(frames, frames, C)
+    grad_bias = grad_bias.reshape(C)
     return (
         grad_input.reshape(1, 4 * pixels, C),
         grad_down,

time: 208 us -> 93.3 us (0.45)
  waiting for transfers between devices: 107 us -> 15.6 us
  blocking collectives: 37.6 us -> 0 us
  Pallas kernels: 0 us -> 27.6 us
  between operations: 14.4 us -> 1.05 us
  other arithmetic: 11.1 us -> 7.79 us
  local copies, waits for them, and re-layouts: 16 us -> 18.2 us
    psum x1 -> x0, waiting for transfers between devices: 89.4 us -> none  [on_device(): lax.psum((terms[0], terms[1], terms[2], terms[3], terms[4]), ('tm', 'pix'))]
    psum x1 -> x0, blocking collectives: 37.6 us -> none  [on_device(): lax.psum((terms[0], terms[1], terms[2], terms[3], terms[4]), ('tm', 'pix'))]
    pallas_call x0 -> x1, Pallas kernels: none -> 27.6 us  [total_over_devices(): pl.pallas_call(functools.partial(total_kernel, rows, scale), out_shape=ou...]
    mul x5 -> x0, other arithmetic: 3.22 us -> none  [the longest x1 1.32 us: on_device(): grad_down = totals[0] * scale]
    ppermute x2, waiting for transfers between devices: 5.16 us -> 2.65 us  [padded_2(): lax.ppermute(tail, axis, [(i, (i + 1) % count) for i in range(count)])]
    unnamed x26 -> x37, local copies, waits for them, and re-layouts: 5.03 us -> 5.74 us
  transfers between devices with their start and end apart: 7 -> 6, of which waited for: 5 -> 4; matrix products, arithmetic and copies ran while one was open for 6% -> 12% of each run, Pallas kernels for 0% -> 0%
where the time goes in v1:
time: 93.3 us; the launch traced here: 92.9 us
  Pallas kernels  27.6 us (30%)
  local copies, waits for them, and re-layouts  18.2 us (20%)
  starting transfers between devices  16.7 us (18%)
  waiting for transfers between devices  15.6 us (17%)
  other arithmetic  7.79 us (8%)
  matrix products  5.91 us (6%)
  between operations  1.05 us (1%)
    pallas_call x1, Pallas kernels, total_over_devices(): pl.pallas_call(functools.partial(total_kernel, rows, scale), out_shape=ou...  27.6 us
    ppermute x2, starting transfers between devices, padded_2(): lax.ppermute(head, axis, [((i + 1) % count, i) for i in range(count)])  9.02 us
    all_to_all x1, waiting for transfers between devices, on_device(): lax.all_to_all(mixed_grad, 'tm', split_axis=0, concat_axis=1, tiled=True)  6.67 us
    all_to_all x1, waiting for transfers between devices, on_device(): lax.all_to_all(mixed_in.reshape(1, pixels, C), 'tm', split_axis=1, concat...  6.29 us
    unnamed x37, local copies, waits for them, and re-layouts  5.74 us
    all_to_all x1, starting transfers between devices, on_device(): lax.all_to_all(mixed_grad, 'tm', split_axis=0, concat_axis=1, tiled=True)  4.24 us
    all_to_all x1, starting transfers between devices, on_device(): lax.all_to_all(mixed_in.reshape(1, pixels, C), 'tm', split_axis=1, concat...  3.45 us
    reshape x1, local copies, waits for them, and re-layouts, on_device(): rows_in = activations.reshape(pixels, 4 * C)  3.38 us
  transfers between devices with their start and end apart: 6, of which 4 were waited for; matrix products, arithmetic and copies ran while one was open for 12% of the time, Pallas kernels for 0%

profile of v1, /device:TPU:0, one launch (start us, length us, event | category | flops | bytes accessed | tf_op | source)
XLA Modules:
  0.0 92.9 jit_solution(14493124695319366305)
XLA Ops:
  0.6 0.8 slice_bitcast_fusion.9
  1.4 1.0 %convert_element_type.87 = f32[4,160,256]{2,1,0:T(8,128)S(1)} convert(bf16[4,160,256]{2,1,0:T(8,128)(2,1)} %param.23) | non-fusion elementwise | flops 163840 | bytes 983040 | tf_op jit(solution)/shard_map/convert_element_type | solution.py:208
  2.6 0.9 add_convert_fusion
  3.5 4.2 %all-to-all-start = ((bf16[4,160,256]{2,1,0:T(8,128)(2,1)}), bf16[4,160,256]{2,1,0:T(8,128)(2,1)S(1)}, u32[]{:S(2)}, u32[]{:S(2)}) async-start(bf16[4,160,256]{2,1,0:T(8,128)(2,1)} %add_convert_fusion), calls=%async_computation | async-start | bytes 655360 | tf_op jit(solution)/shard_map/all_to_all | solution.py:213
  7.8 6.7 %all-to-all-done = bf16[4,160,256]{2,1,0:T(8,128)(2,1)S(1)} async-done(((bf16[4,160,256]{2,1,0:T(8,128)(2,1)}), bf16[4,160,256]{2,1,0:T(8,128)(2,1)S(1)}, u32[]{:S(2)}, u32[]{:S(2)}) %all-to-all-start) | async-done | bytes 327712 | tf_op jit(solution)/shard_map/all_to_all | solution.py:213
  16.4 5.2 %collective-permute-start.1 = (bf16[20,1,256]{2,0,1:T(8,128)(2,1)S(1)}, bf16[20,1,256]{2,0,1:T(8,128)(2,1)S(1)}, u32[]{:S(2)}, u32[]{:S(2)}) collective-permute-start(bf16[20,1,256]{2,0,1:T(8,128)(2,1)S(1)} %fusion.49), channel_id=1, source_target_pairs={{1,0},{2,1},{3,2},{4,3},{5,4},{6,5},{7,6},{0,7},{9,8},{10,9},{11,1... | collective-permute-start | bytes 30728 | tf_op jit(solution)/shard_map/ppermute | solution.py:26
  22.2 1.1 %copy.50 = bf16[4,160,256]{1,0,2:T(4,128)(2,1)} copy(bf16[4,160,256]{2,1,0:T(8,128)(2,1)S(1)} %copy-done.2) | data formatting | bytes 655360 | tf_op args[7]
  23.3 3.4 %reshape.139 = bf16[640,1024]{1,0:T(8,128)(2,1)} reshape(bf16[1,2560,256]{2,1,0:T(8,128)(2,1)} %param.16) | data formatting | bytes 2621440 | tf_op jit(solution)/shard_map/reshape | solution.py:180
  26.8 1.9 %collective-permute-done = bf16[20,1,256]{2,0,1:T(8,128)(2,1)S(1)} collective-permute-done((bf16[20,1,256]{2,0,1:T(8,128)(2,1)S(1)}, bf16[20,1,256]{2,0,1:T(8,128)(2,1)S(1)}, u32[]{:S(2)}, u32[]{:S(2)}) %collective-permute-start) | collective-permute-done | bytes 10272 | tf_op jit(solution)/shard_map/ppermute | solution.py:24
  28.9 1.3 %fusion.38 = (f32[256]{0:T(256)}, bf16[640,256]{1,0:T(8,128)(2,1)S(1)}, f32[256]{0:T(256)S(1)}, bf16[640,256]{1,0:T(8,128)(2,1)S(1)}) fusion(f32[640,256]{1,0:T(8,128)S(1)} %fusion.1, f32[20,32,256]{2,1,0:T(8,128)S(1)} %copy.40, bf16[4,160,256]{2,1,0:T(8,128)(2,1)S(1)} %all-to-all-done, f32[256]{0:T(256)S(1)} %copy-done.12, ...), kind=kOutput, calls=%fused_computation.76 | convolution fusion | flops 338656768 | bytes 4131840 | tf_op jit(solution)/shard_map/dot_general | solution.py:181
  31.0 3.9 %collective-permute-start.3 = (bf16[1,20,1,256]{3,1,2,0:T(8,128)(2,1)S(1)}, bf16[1,20,1,256]{3,1,2,0:T(8,128)(2,1)S(1)}, u32[]{:S(2)}, u32[]{:S(2)}) collective-permute-start(bf16[1,20,1,256]{3,1,2,0:T(8,128)(2,1)S(1)} %copy.55), channel_id=1, source_target_pairs={{1,0},{2,1},{3,2},{4,3},{5,4},{6,5},{7,6},{0,7},{9,8},{10,9},{11,1... | collective-permute-start | bytes 30728 | tf_op jit(solution)/shard_map/ppermute | solution.py:26
  34.9 1.6 %convolution_convert_fusion = bf16[640,1024]{1,0:T(8,128)(2,1)} fusion(bf16[640,256]{1,0:T(8,128)(2,1)S(1)} %get-tuple-element.63, bf16[1024,256]{1,0:T(8,128)(2,1)S(1)} %copy-done), kind=kOutput, calls=%fused_computation.4 | convolution fusion | flops 336199680 | bytes 2162688 | tf_op jit(solution)/shard_map/dot_general | solution.py:251
  36.5 3.4 %reshape.140 = bf16[1,2560,256]{2,1,0:T(8,128)(2,1)} reshape(bf16[640,1024]{1,0:T(8,128)(2,1)} %convolution_convert_fusion) | data formatting | bytes 2621440 | tf_op jit(solution)/shard_map/reshape | solution.py:266
  40.5 0.8 collective-permute-done.2
  42.2 1.3 %fusion.37 = (f32[256]{0:T(256)S(1)}, f32[256]{0:T(256)S(1)}, f32[256]{0:T(256)S(1)}, f32[256]{0:T(256)}, f32[256]{0:T(256)}, /*index=5*/f32[256]{0:T(256)}, f32[256]{0:T(256)}, f32[256]{0:T(256)}) fusion(f32[20,32,256]{2,1,0:T(8,128)S(1)} %bitcast.98, bf16[22,34,256]{2,1,0:T(8,128)(2,1)S(1)} %fusion.45, bf16[20,32,256]{2,1,0:T(8,128)(2,1)S(1)} %bitcast.101, ...), kind=kLoop, calls=%fused_computation.75 | loop fusion | flops 4913152 | bytes 2977792 | tf_op jit(solution)/shard_map/reduce_sum | solution.py:224
  43.6 0.8 fusion.29
  45.7 2.7 %reduce.5 = bf16[640,256]{1,0:T(8,128)(2,1)S(1)} reduce(bf16[640,1,256]{2,1,0:T(2,128)(2,1)S(1)} %bitcast.107, bf16[]{:T(256)} %broadcast.131), dimensions={1}, to_apply=%bitcast.94.reduce_sub_computation | reduce | bytes 655362
  48.5 0.8 reshape.193
  49.3 3.5 %all-to-all-start.1 = ((bf16[4,2,20480]{2,1,0:T(2,128)(2,1)}), bf16[4,2,20480]{2,1,0:T(2,128)(2,1)S(1)}, u32[]{:S(2)}, u32[]{:S(2)}) async-start(bf16[4,2,20480]{2,1,0:T(2,128)(2,1)} %reshape.193), calls=%async_computation.1 | async-start | bytes 655360 | tf_op jit(solution)/shard_map/all_to_all | solution.py:204
  53.1 6.3 %all-to-all-done.1 = bf16[4,2,20480]{2,1,0:T(2,128)(2,1)S(1)} async-done(((bf16[4,2,20480]{2,1,0:T(2,128)(2,1)}), bf16[4,2,20480]{2,1,0:T(2,128)(2,1)S(1)}, u32[]{:S(2)}, u32[]{:S(2)}) %all-to-all-start.1) | async-done | bytes 327712 | tf_op jit(solution)/shard_map/all_to_all | solution.py:204
  60.1 1.5 %convolution_bitcast_fusion.1 = f32[4,4,256]{0,1,2:T(4,128)S(1)} fusion(bf16[4,160,256]{1,0,2:T(4,128)(2,1)S(1)} %copy.49, bf16[4,160,256]{1,0,2:T(4,128)(2,1)} %copy.50), kind=kOutput, calls=%fused_computation.10 | convolution fusion | flops 1310720 | bytes 671744 | tf_op jit(solution)/shard_map/gpc,fpc->fgc/dot_general | solution.py:207
  61.8 27.6 %shard_map.127 = (f32[1024,256]{1,0:T(8,128)S(1)}, f32[256,256]{1,0:T(8,128)S(1)}, f32[9,256]{1,0:T(8,128)S(1)}, f32[16,256]{1,0:T(8,128)S(1)}, f32[1,256]{1,0:T(1,128)S(1)}) custom-call(f32[1024,256]{1,0:T(8,128)S(1)} %convolution_bitcast_fusion.down, f32[256,256]{1,0:T(8,128)S(1)} %fusion.53.point, f32[9,256]{1,0:T(8,128)S(1)} %stack.51.taps, ...), custom_call_target="tpu_custom_call" | custom-call | tf_op jit(solution)/shard_map/pallas_call | solution.py:151
  90.0 1.0 %copy.64 = f32[1024,256]{1,0:T(8,128)} copy(f32[1024,256]{1,0:T(8,128)S(1)} %get-tuple-element.94) | data formatting | bytes 2097152
  92.2 0.7 copy.67
  (70 shorter events, 9.7 us)
Async XLA Ops:
  0.6 28.2 %copy-start = (bf16[1024,256]{1,0:T(8,128)(2,1)S(1)}, bf16[1024,256]{1,0:T(8,128)(2,1)}, u32[]{:S(2)}) copy-start(bf16[1024,256]{1,0:T(8,128)(2,1)} %param.17) | copy-start | bytes 1572868
  2.5 5.2 %copy-start.10 = (s32[1,2,20]{2,1,0:T(2,128)S(1)}, s32[1,2,20]{2,1,0:T(2,128)}, u32[]{:S(2)}) copy-start(s32[1,2,20]{2,1,0:T(2,128)} %param.22) | copy-start | bytes 484
  2.5 5.3 %copy-start.4 = (f32[9,256]{1,0:T(8,128)S(1)}, f32[9,256]{1,0:T(8,128)}, u32[]{:S(2)}) copy-start(f32[9,256]{1,0:T(8,128)} %param.19) | copy-start | bytes 27652
  2.5 11.9 %copy-start.3 = (bf16[256,256]{1,0:T(8,128)(2,1)S(1)}, bf16[256,256]{1,0:T(8,128)(2,1)}, u32[]{:S(2)}) copy-start(bf16[256,256]{1,0:T(8,128)(2,1)} %param.20) | copy-start | bytes 393220
  3.5 11.0 %all-to-all-start = ((bf16[4,160,256]{2,1,0:T(8,128)(2,1)}), bf16[4,160,256]{2,1,0:T(8,128)(2,1)S(1)}, u32[]{:S(2)}, u32[]{:S(2)}) async-start(bf16[4,160,256]{2,1,0:T(8,128)(2,1)} %add_convert_fusion), calls=%async_computation | async-start | bytes 655360 | tf_op jit(solution)/shard_map/all_to_all | solution.py:213
  15.1 7.1 %copy-start.2 = (bf16[4,160,256]{2,1,0:T(8,128)(2,1)S(1)}, bf16[4,160,256]{2,1,0:T(8,128)(2,1)}, u32[]{:S(2)}) copy-start(bf16[4,160,256]{2,1,0:T(8,128)(2,1)} %param.23) | copy-start | bytes 983044
  16.4 10.4 %collective-permute-start.1 = (bf16[20,1,256]{2,0,1:T(8,128)(2,1)S(1)}, bf16[20,1,256]{2,0,1:T(8,128)(2,1)S(1)}, u32[]{:S(2)}, u32[]{:S(2)}) collective-permute-start(bf16[20,1,256]{2,0,1:T(8,128)(2,1)S(1)} %fusion.49), channel_id=1, source_target_pairs={{1,0},{2,1},{3,2},{4,3},{5,4},{6,5},{7,6},{0,7},{9,8},{10,9},{11,1... | collective-permute-start | bytes 30728 | tf_op jit(solution)/shard_map/ppermute | solution.py:26
  22.2 6.4 %collective-permute-start = (bf16[20,1,256]{2,0,1:T(8,128)(2,1)S(1)}, bf16[20,1,256]{2,0,1:T(8,128)(2,1)S(1)}, u32[]{:S(2)}, u32[]{:S(2)}) collective-permute-start(bf16[20,1,256]{2,0,1:T(8,128)(2,1)S(1)} %fusion.48), channel_id=1, source_target_pairs={{0,1},{1,2},{2,3},{3,4},{4,5},{5,6},{6,7},{7,0},{8,9},{9,10},{10,1... | collective-permute-start | bytes 30728 | tf_op jit(solution)/shard_map/ppermute | solution.py:24
  26.7 2.2 %copy-start.1 = (bf16[640,1024]{1,0:T(8,128)(2,1)S(1)}, bf16[640,1024]{1,0:T(8,128)(2,1)}, u32[]{:S(2)}) copy-start(bf16[640,1024]{1,0:T(8,128)(2,1)} %reshape.139) | copy-start | bytes 3932164
  26.7 2.2 %copy-start.12 = (f32[256]{0:T(256)S(1)}, f32[256]{0:T(256)}, u32[]{:S(2)}) copy-start(f32[256]{0:T(256)} %param.18) | copy-start | bytes 3076
  31.0 8.9 %collective-permute-start.3 = (bf16[1,20,1,256]{3,1,2,0:T(8,128)(2,1)S(1)}, bf16[1,20,1,256]{3,1,2,0:T(8,128)(2,1)S(1)}, u32[]{:S(2)}, u32[]{:S(2)}) collective-permute-start(bf16[1,20,1,256]{3,1,2,0:T(8,128)(2,1)S(1)} %copy.55), channel_id=1, source_target_pairs={{1,0},{2,1},{3,2},{4,3},{5,4},{6,5},{7,6},{0,7},{9,8},{10,9},{11,1... | collective-permute-start | bytes 30728 | tf_op jit(solution)/shard_map/ppermute | solution.py:26
  34.9 6.4 %collective-permute-start.2 = (bf16[1,20,1,256]{3,1,2,0:T(8,128)(2,1)S(1)}, bf16[1,20,1,256]{3,1,2,0:T(8,128)(2,1)S(1)}, u32[]{:S(2)}, u32[]{:S(2)}) collective-permute-start(bf16[1,20,1,256]{3,1,2,0:T(8,128)(2,1)S(1)} %copy.54), channel_id=1, source_target_pairs={{0,1},{1,2},{2,3},{3,4},{4,5},{5,6},{6,7},{7,0},{8,9},{9,10},{10,1... | collective-permute-start | bytes 30728 | tf_op jit(solution)/shard_map/ppermute | solution.py:24
  45.1 7.7 %copy-start.5 = (f32[256]{0:T(256)S(1)}, f32[256]{0:T(256)}, u32[]{:S(2)}) copy-start(f32[256]{0:T(256)} %get-tuple-element.45) | copy-start | bytes 3076
  45.1 7.7 %copy-start.6 = (f32[256]{0:T(256)S(1)}, f32[256]{0:T(256)}, u32[]{:S(2)}) copy-start(f32[256]{0:T(256)} %get-tuple-element.46) | copy-start | bytes 3076
  45.1 7.6 %copy-start.7 = (f32[256]{0:T(256)S(1)}, f32[256]{0:T(256)}, u32[]{:S(2)}) copy-start(f32[256]{0:T(256)} %get-tuple-element.47) | copy-start | bytes 3076
  45.1 7.6 %copy-start.8 = (f32[256]{0:T(256)S(1)}, f32[256]{0:T(256)}, u32[]{:S(2)}) copy-start(f32[256]{0:T(256)} %get-tuple-element.50) | copy-start | bytes 3076
  45.1 7.6 %copy-start.9 = (f32[256]{0:T(256)S(1)}, f32[256]{0:T(256)}, u32[]{:S(2)}) copy-start(f32[256]{0:T(256)} %get-tuple-element.51) | copy-start | bytes 3076
  45.1 7.6 %copy-start.11 = (f32[256]{0:T(256)S(1)}, f32[256]{0:T(256)}, u32[]{:S(2)}) copy-start(f32[256]{0:T(256)} %get-tuple-element.54) | copy-start | bytes 3076
  49.3 10.2 %all-to-all-start.1 = ((bf16[4,2,20480]{2,1,0:T(2,128)(2,1)}), bf16[4,2,20480]{2,1,0:T(2,128)(2,1)S(1)}, u32[]{:S(2)}, u32[]{:S(2)}) async-start(bf16[4,2,20480]{2,1,0:T(2,128)(2,1)} %reshape.193), calls=%async_computation.1 | async-start | bytes 655360 | tf_op jit(solution)/shard_map/all_to_all | solution.py:204

commit v2 on v1

v2 whole, which is shorter than its diff:
```python
import functools
import math

import jax
import jax.numpy as jnp
from jax import lax
from jax.experimental import pallas as pl
from jax.experimental.pallas import tpu as pltpu
from jax.sharding import PartitionSpec as P

C = 256
TR = 20
TC = 32
MESH = pl.DeviceIdType.MESH


def kernel(
    rows, scale, act, weight, bias, taps, point, mix, perm, cot,
    out_input, out_down, out_bias, out_taps, out_point, out_mix,
    fine, rows_in, rows_t, preact, pooled, wide, gwide, grad, spread, mixed_low,
    mg_send, mg_recv, mix_send, mix_recv, edge, edge_send, edge_recv, back_send, back_recv, pre,
    packed, core_in, half, parts, mine, gathered, other,
    mg_sems, mix_sems, edge_sems, back_sems,
    core_sems, part_send, part_recv, all_send, all_recv, pair_send, pair_recv,
):
    f32, low = jnp.float32, jnp.bfloat16
    tm, pix = lax.axis_index("tm"), lax.axis_index("pix")
    n_tm, n_pix = lax.axis_size("tm"), lax.axis_size("pix")
    group = n_tm // 2 * n_pix
    core = lax.rem(tm, 2)
    me = tm // 2 * n_pix + pix
    partner = (tm + 1 - 2 * core, pix)
    west, east = (tm, lax.rem(pix + n_pix - 1, n_pix)), (tm, lax.rem(pix + 1, n_pix))
    quarter = TR * TC // n_tm

    def peer(step):
        index = lax.rem(me + step, group)
        return index, (index // n_pix * 2 + core, lax.rem(index, n_pix))

    barrier = pltpu.get_barrier_semaphore()
    pl.semaphore_signal(barrier, inc=1, device_id=partner, device_id_type=MESH)
    across = (lax.rem(partner[0] + 2, n_tm), pix)
    pl.semaphore_signal(barrier, inc=1, device_id=across, device_id_type=MESH)

    @pl.loop(1, group)
    def _(step):
        _, device = peer(step)
        pl.semaphore_signal(barrier, inc=1, device_id=device, device_id_type=MESH)

    for frame in range(n_tm):
        total = mix[frame : frame + 1] * cot[0].astype(f32)
        for source in range(1, n_tm):
            total = total + mix[n_tm * source + frame : n_tm * source + frame + 1] * cot[
                source
            ].astype(f32)
        mg_send[frame] = total.astype(low)
    pl.semaphore_wait(barrier, group + 1)

    def exchange(send, recv, sems, step):
        target = lax.rem(tm + step, n_tm)
        return pltpu.make_async_remote_copy(
            send.at[target], recv.at[tm], sems.at[0, step], sems.at[1, step], (target, pix), MESH
        )

    for step in range(1, n_tm):
        exchange(mg_send, mg_recv, mg_sems, step).start()
    mg_recv[tm] = mg_send[tm]

    @pl.loop(0, 2560 // 160)
    def _(i):
        at = pl.ds(pl.multiple_of(i * 160, 160), 160)
        for side in range(2):
            fine[side, at, :] = act[at, side * 128 : side * 128 + 128].astype(f32)

    for child in range(4):
        for side in range(2):
            lanes = slice(child * C + side * 128, child * C + side * 128 + 128)
            rows_in[:, lanes] = fine[side, pl.ds(child, TR * TC, stride=4), :].astype(low)

    @pl.loop(0, 4)
    def _(i):
        at = pl.ds(pl.multiple_of(i * 160, 160), 160)
        value = jnp.dot(rows_in[at, :], weight[...], preferred_element_type=f32) + bias[...]
        preact[at, :] = value
        pooled[at, :] = (value / (1.0 + jnp.exp(-value))).astype(low)

    def shifted(ref, values, r):
        ref[1, r + 1] = values
        ref[0, r + 1, 1:TC, :] = values[0 : TC - 1]
        ref[2, r + 1, 0 : TC - 1, :] = values[1:TC]

    for side in range(3):
        for r in (0, TR + 1):
            wide[side, r] = jnp.zeros((TC, C), f32)
            gwide[side, r] = jnp.zeros((TC, C), f32)

    @pl.loop(0, TR)
    def _(r):
        shifted(wide, pooled[pl.ds(pl.multiple_of(r * TC, TC), TC), :].astype(f32), r)

    edge[...] = jnp.zeros(edge.shape, f32)
    for r in range(TR):
        edge[0, r : r + 1] = wide[1, r + 1, 0:1, :]
        edge[1, r : r + 1] = wide[1, r + 1, TC - 1 : TC, :]
    edge_send[...] = edge[...].astype(low)

    def swap_edges(send, recv, sems):
        return [
            pltpu.make_async_remote_copy(
                send.at[0], recv.at[1], sems.at[0, 0], sems.at[1, 0], west, MESH
            ),
            pltpu.make_async_remote_copy(
                send.at[1], recv.at[0], sems.at[0, 1], sems.at[1, 1], east, MESH
            ),
        ]

    forward = swap_edges(edge_send, edge_recv, edge_sems)
    for copy in forward:
        copy.start()

    for child in range(4):
        lanes = slice(child * C, child * C + C)
        rows_t[lanes, :] = rows_in[:, lanes].T

    for step in range(1, n_tm):
        exchange(mg_send, mg_recv, mg_sems, step).wait()

    @pl.loop(0, n_tm)
    def _(i):
        value = lax.dot_general(
            mg_recv[i], point[...], (((1,), (1,)), ((), ())), preferred_element_type=f32
        )
        pre[pl.ds(pl.multiple_of(i * quarter, quarter), quarter), :] = value.astype(low)

    @pl.loop(0, TR)
    def _(r):
        shifted(gwide, pre[pl.ds(pl.multiple_of(r * TC, TC), TC), :].astype(f32), r)
        gwide[0, r + 1, 0:1, :] = jnp.zeros((1, C), f32)
        gwide[2, r + 1, TC - 1 : TC, :] = jnp.zeros((1, C), f32)

    edge[...] = jnp.zeros(edge.shape, f32)
    for r in range(TR):
        edge[0, r + 1 : r + 2] = gwide[1, r + 1, 0:1, :]
        edge[1, r + 1 : r + 2] = gwide[1, r + 1, TC - 1 : TC, :]
    for side in range(2):
        total = jnp.zeros((TR, C), f32)
        for a in range(3):
            tap = 3 * a + 2 * side
            total = total + taps[tap : tap + 1] * edge[side, 2 - a : 2 - a + TR]
        total = jnp.concatenate([total, jnp.zeros((32 - TR, C), f32)], axis=0).astype(low)
        back_send[side] = jnp.dot(perm[side], total, preferred_element_type=f32).astype(low)
    backward = swap_edges(back_send, back_recv, back_sems)
    for copy in backward:
        copy.start()

    for copy in forward:
        copy.wait()
    for side in range(2):
        edge[side] = jnp.dot(perm[side], edge_recv[side], preferred_element_type=f32)
    for r in range(TR):
        wide[0, r + 1, 0:1, :] = edge[0, r : r + 1]
        wide[2, r + 1, TC - 1 : TC, :] = edge[1, r : r + 1]

    def conv(r, sums):
        total = jnp.zeros((TC, C), f32)
        inner = mg_recv[r // (TR // n_tm), pl.ds(
            pl.multiple_of(lax.rem(r, TR // n_tm) * TC, TC), TC
        ), :].astype(f32)
        here = gwide[1, r + 1]
        new = []
        for a in range(3):
            for b in range(3):
                tap = taps[3 * a + b : 3 * a + b + 1]
                cells = wide[b, r + a]
                total = total + tap * cells
                inner = inner + tap * gwide[2 - b, r + 2 - a]
                product = here * cells
                new.append(
                    sums[3 * a + b]
                    + ((product[0:8] + product[8:16]) + (product[16:24] + product[24:32]))
                )
        at = pl.ds(pl.multiple_of(r * TC, TC), TC)
        spread[at, :] = total.astype(low)
        grad[at, :] = inner
        return tuple(new)

    sums = lax.fori_loop(0, TR, conv, tuple(jnp.zeros((8, C), f32) for _ in range(9)))
    taps_part = [jnp.sum(x, axis=0, keepdims=True) for x in sums]

    @pl.loop(0, n_tm)
    def _(i):
        at = pl.ds(pl.multiple_of(i * quarter, quarter), quarter)
        value = jnp.dot(spread[at, :], point[...], preferred_element_type=f32)
        mix_send[i] = (pooled[at, :].astype(f32) + value).astype(low)
        mixed_low[at, :] = mg_recv[i]

    for step in range(1, n_tm):
        exchange(mix_send, mix_recv, mix_sems, step).start()
    mix_recv[tm] = mix_send[tm]

    def pack(first, value):
        for side in range(2):
            packed[side, first : first + value.shape[0], :] = value[
                :, side * 128 : side * 128 + 128
            ].astype(low)

    across_rows = (((0,), (0,)), ((), ()))
    pack(4 * C, lax.dot_general(spread[...], mixed_low[...], across_rows, preferred_element_type=f32))

    for copy in backward:
        copy.wait()
    edge[...] = back_recv[...].astype(f32)
    for r in range(TR):
        grad[r * TC : r * TC + 1, :] += edge[0, r : r + 1]
        grad[r * TC + TC - 1 : r * TC + TC, :] += edge[1, r : r + 1]

    def through(r, total):
        at = pl.ds(pl.multiple_of(r * TC, TC), TC)
        value = preact[at, :]
        sigma = 1.0 / (1.0 + jnp.exp(-value))
        low_grad = (grad[at, :] * (sigma * (1.0 + value * (1.0 - sigma)))).astype(low)
        pre[at, :] = low_grad
        wider = low_grad.astype(f32)
        return total + ((wider[0:8] + wider[8:16]) + (wider[16:24] + wider[24:32]))

    bias_part = lax.fori_loop(0, TR, through, jnp.zeros((8, C), f32))
    for child in range(4):
        lanes = slice(child * C, child * C + C)
        pack(child * C, jnp.dot(rows_t[lanes, :], pre[...], preferred_element_type=f32))

    for step in range(1, n_tm):
        exchange(mix_send, mix_recv, mix_sems, step).wait()

    def mixing(i, sums):
        at = pl.ds(pl.multiple_of(i * 16, 16), 16)
        cots = [cot[f, at, :].astype(f32) for f in range(n_tm)]
        mixes = [mix_recv[g, at, :].astype(f32) for g in range(n_tm)]
        new = []
        for f in range(n_tm):
            for g in range(n_tm):
                product = cots[f] * mixes[g]
                new.append(sums[n_tm * f + g] + (product[0:8] + product[8:16]))
        return tuple(new)

    sums = lax.fori_loop(
        0, quarter // 16, mixing, tuple(jnp.zeros((8, C), f32) for _ in range(n_tm * n_tm))
    )
    small = taps_part + [jnp.sum(x, axis=0, keepdims=True) for x in sums]
    small.append(jnp.sum(bias_part, axis=0, keepdims=True))
    small.append(jnp.zeros((6, C), f32))
    pack(5 * C, jnp.concatenate(small, axis=0))
    for side in range(2):
        packed[side, 1312:, :] = jnp.zeros((group * rows - 1312, 128), low)

    swap = pltpu.make_async_remote_copy(
        packed.at[1 - core], core_in, core_sems.at[0], core_sems.at[1], partner, MESH
    )
    swap.start()
    swap.wait()
    half[...] = (packed[core].astype(f32) + core_in[...].astype(f32)).astype(low)

    def send_part(step):
        index, device = peer(step)
        return pltpu.make_async_remote_copy(
            half.at[pl.ds(pl.multiple_of(index * rows, 16), rows)],
            parts.at[step], part_send.at[step], part_recv.at[step], device, MESH
        )

    @pl.loop(1, group)
    def _(step):
        send_part(step).start()

    parts[0] = half[pl.ds(pl.multiple_of(me * rows, 16), rows), :]

    for child in range(4):
        lanes = slice(child * C, child * C + C)
        value = lax.dot_general(
            pre[...], weight[lanes, :], (((1,), (1,)), ((), ())), preferred_element_type=f32
        )
        for side in range(2):
            fine[side, pl.ds(child, TR * TC, stride=4), :] = value[:, side * 128 : side * 128 + 128]

    @pl.loop(0, 2560 // 160)
    def _(i):
        at = pl.ds(pl.multiple_of(i * 160, 160), 160)
        for side in range(2):
            out_input[at, side * 128 : side * 128 + 128] = fine[side, at, :].astype(low)

    @pl.loop(1, group)
    def _(step):
        send_part(step).wait()

    def add(step, total):
        return total + parts[step].astype(f32)

    mine[...] = lax.fori_loop(0, group, add, jnp.zeros((rows, 128), f32)).astype(low)

    def send_all(step):
        _, device = peer(step)
        return pltpu.make_async_remote_copy(
            mine, gathered.at[step], all_send.at[step], all_recv.at[step], device, MESH
        )

    def send_pair(step):
        return pltpu.make_async_remote_copy(
            gathered.at[step], other.at[step], pair_send.at[step], pair_recv.at[step], partner, MESH
        )

    @pl.loop(1, group)
    def _(step):
        send_all(step).start()

    gathered[0] = mine[...]
    send_pair(0).start()

    @pl.loop(1, group)
    def _(step):
        send_all(step).wait()
        send_pair(step).start()

    @pl.loop(0, group)
    def _(step):
        send_pair(step).wait()

    @pl.loop(0, group)
    def _(step):
        index = lax.rem(me + group - step, group)
        place = pl.ds(pl.multiple_of(index * rows, 16), rows)
        packed[core, place, :] = gathered[step]
        packed[1 - core, place, :] = other[step]

    for side in range(2):
        lanes = slice(side * 128, side * 128 + 128)
        out_down[:, lanes] = packed[side, 0:1024, :].astype(f32) * scale
        out_point[:, lanes] = packed[side, 1024:1280, :].astype(f32) * scale
        tail = packed[side, 1280:1312, :].astype(f32) * scale
        out_taps[:, lanes] = tail[0:9]
        out_mix[:, lanes] = tail[9:25]
        out_bias[:, lanes] = tail[25:26]


def on_device(
    activations, down_weight, down_bias, taps, point_weight, time_mix, edge_rows, cotangent
):
    frames = lax.axis_size("tm")
    tiles = lax.axis_size("pix")
    pixels = TR * TC
    quarter = pixels // frames
    scale = 1.0 / math.sqrt(frames * tiles * pixels)
    group = frames // 2 * tiles
    rows = -(-1312 // (16 * group)) * 16
    f32, low = jnp.float32, jnp.bfloat16
    sems = pltpu.SemaphoreType.DMA((group,))
    both = lambda n: pltpu.SemaphoreType.DMA((2, n))
    place = lax.broadcasted_iota(jnp.int32, (2, 32, 32), 2)
    maps = jnp.pad(edge_rows[0], ((0, 0), (0, 32 - TR)), constant_values=-1)
    perm = (maps[:, :, None] == place).astype(low)
    vmem = pl.BlockSpec(memory_space=pltpu.VMEM)
    outs = pl.pallas_call(
        functools.partial(kernel, rows, scale),
        out_shape=[
            jax.ShapeDtypeStruct((4 * pixels, C), low),
            jax.ShapeDtypeStruct((4 * C, C), f32),
            jax.ShapeDtypeStruct((1, C), f32),
            jax.ShapeDtypeStruct((9, C), f32),
            jax.ShapeDtypeStruct((C, C), f32),
            jax.ShapeDtypeStruct((frames * frames, C), f32),
        ],
        in_specs=[vmem] * 8,
        out_specs=[vmem] * 6,
        scratch_shapes=[
            pltpu.VMEM((2, 4 * pixels, 128), f32),
            pltpu.VMEM((pixels, 4 * C), low),
            pltpu.VMEM((4 * C, pixels), low),
            pltpu.VMEM((pixels, C), f32),
            pltpu.VMEM((pixels, C), low),
            pltpu.VMEM((3, TR + 2, TC, C), f32),
            pltpu.VMEM((3, TR + 2, TC, C), f32),
            pltpu.VMEM((pixels, C), f32),
            pltpu.VMEM((pixels, C), low),
            pltpu.VMEM((pixels, C), low),
            pltpu.VMEM((frames, quarter, C), low),
            pltpu.VMEM((frames, quarter, C), low),
            pltpu.VMEM((frames, quarter, C), low),
            pltpu.VMEM((frames, quarter, C), low),
            pltpu.VMEM((2, 32, C), f32),
            pltpu.VMEM((2, 32, C), low),
            pltpu.VMEM((2, 32, C), low),
            pltpu.VMEM((2, 32, C), low),
            pltpu.VMEM((2, 32, C), low),
            pltpu.VMEM((pixels, C), low),
            pltpu.VMEM((2, group * rows, 128), low),
            pltpu.VMEM((group * rows, 128), low),
            pltpu.VMEM((group * rows, 128), low),
            pltpu.VMEM((group, rows, 128), low),
            pltpu.VMEM((rows, 128), low),
            pltpu.VMEM((group, rows, 128), low),
            pltpu.VMEM((group, rows, 128), low),
            both(frames), both(frames), both(2), both(2),
            pltpu.SemaphoreType.DMA((2,)),
            sems, sems, sems, sems, sems, sems,
        ],
        compiler_params=pltpu.CompilerParams(
            collective_id=0, has_side_effects=True, vmem_limit_bytes=48 * 1024 * 1024
        ),
    )(
        activations.reshape(4 * pixels, C),
        down_weight,
        down_bias.reshape(1, C),
        taps,
        point_weight,
        time_mix.reshape(frames * frames, C),
        perm,
        cotangent,
    )
    return (
        outs[0].reshape(1, 4 * pixels, C),
        outs[1],
        outs[2].reshape(C),
        outs[3],
        outs[4],
        outs[5].reshape(frames, frames, C),
    )


def solution(mesh):
    in_specs = (
        P("tm", "pix", None),
        P(),
        P(),
        P(),
        P(),
        P(),
        P("pix", None, None),
        P(None, ("pix", "tm"), None),
    )
    out_specs = (P("tm", "pix", None), P(), P(), P(), P(), P())
    return jax.shard_map(
        on_device, mesh=mesh, in_specs=in_specs, out_specs=out_specs, check_vma=False
    )
```

time: 93.3 us -> 56.1 us (0.60)
  starting transfers between devices: 16.7 us -> 0 us
  Pallas kernels: 27.6 us -> 43.4 us
  waiting for transfers between devices: 15.6 us -> 0 us
  other arithmetic: 7.79 us -> 0.08 us
  local copies, waits for them, and re-layouts: 18.2 us -> 11.6 us
  matrix products: 5.91 us -> 0 us
    pallas_call x1, Pallas kernels: 27.6 us -> 43.4 us  [on_device(): pl.pallas_call(functools.partial(kernel, rows, scale), out_shape=[jax.Sha...]
    all_to_all x2 -> x0, waiting for transfers between devices: 13 us -> none  [the longest x1 6.67 us: on_device(): lax.all_to_all(mixed_grad, 'tm', split_axis=0, concat_axis=1, tiled=True)]
    ppermute x4 -> x0, starting transfers between devices: 9.03 us -> none  [the longest x2 9.02 us: padded_2(): lax.ppermute(head, axis, [((i + 1) % count, i) for i in range(count)])]
    all_to_all x2 -> x0, starting transfers between devices: 7.69 us -> none  [the longest x1 4.24 us: on_device(): lax.all_to_all(mixed_grad, 'tm', split_axis=0, concat_axis=1, tiled=True)]
    reshape x5 -> x2, local copies, waits for them, and re-layouts: 7.9 us -> 1.35 us  [the longest x1 0.73 us: on_device(): time_mix.reshape(frames * frames, C)]
    dot_general x7 -> x0, matrix products: 5.91 us -> none  [the longest x1 1.6 us: on_device(): jnp.dot(pre_grad, down_weight.T, preferred_element_type=jnp.float32)]
    unnamed x37 -> x17, local copies, waits for them, and re-layouts: 5.74 us -> 9.52 us
    unnamed x1 -> x0, other arithmetic: 2.74 us -> none
  transfers between devices with their start and end apart: 6 -> 0, of which waited for: 4 -> 0; matrix products, arithmetic and copies ran while one was open for 12% -> 0% of each run, Pallas kernels for 0% -> 0%
where the time goes in v2:
time: 56.1 us; the launch traced here: 55.7 us
  Pallas kernels  43.4 us (77%)
  local copies, waits for them, and re-layouts  11.6 us (21%)
  between operations  0.65 us (1%)
    pallas_call x1, Pallas kernels, on_device(): pl.pallas_call(functools.partial(kernel, rows, scale), out_shape=[jax.Sha...  43.4 us
    unnamed x17, local copies, waits for them, and re-layouts  9.52 us

profile of v2, /device:TPU:0, one launch (start us, length us, event | category | flops | bytes accessed | tf_op | source)
XLA Modules:
  0.0 55.7 jit_solution(1643886188814439711)
XLA Ops:
  0.6 0.7 %pad.4 = s32[2,32]{1,0:T(2,128)S(1)} pad(s32[2,20]{1,0:T(2,128)} %bitcast.9, s32[]{:T(128)} %constant.0.clone.1), padding=0_0x0_12 | pad | bytes 420 | tf_op jit(solution)/shard_map/jit(_pad)/pad | solution.py:356
  1.3 0.1 fusion.perm
  1.4 0.7 %reshape.33.mix = f32[16,256]{1,0:T(8,128)S(1)} reshape(f32[4,4,256]{2,1,0:T(4,128)} %param.13) | data formatting | bytes 32768 | tf_op jit(solution)/shard_map/reshape | solution.py:412
  2.1 0.0 copy-start
  2.1 1.3 %copy-done = bf16[1,2560,256]{2,1,0:T(8,128)(2,1)S(1)} copy-done((bf16[1,2560,256]{2,1,0:T(8,128)(2,1)S(1)}, bf16[1,2560,256]{2,1,0:T(8,128)(2,1)}, u32[]{:S(2)}) %copy-start) | copy-done | bytes 1310744
  3.4 0.0 copy-start.1
  3.4 1.0 %copy-done.1 = bf16[1024,256]{1,0:T(8,128)(2,1)S(1)} copy-done((bf16[1024,256]{1,0:T(8,128)(2,1)S(1)}, bf16[1024,256]{1,0:T(8,128)(2,1)}, u32[]{:S(2)}) %copy-start.1) | copy-done | bytes 524312
  4.5 0.0 copy-start.2
  4.5 1.0 %copy-done.2 = bf16[4,160,256]{2,1,0:T(8,128)(2,1)S(1)} copy-done((bf16[4,160,256]{2,1,0:T(8,128)(2,1)S(1)}, bf16[4,160,256]{2,1,0:T(8,128)(2,1)}, u32[]{:S(2)}) %copy-start.2) | copy-done | bytes 327704
  5.5 0.0 copy-start.3
  5.5 0.9 %copy-done.3 = bf16[256,256]{1,0:T(8,128)(2,1)S(1)} copy-done((bf16[256,256]{1,0:T(8,128)(2,1)S(1)}, bf16[256,256]{1,0:T(8,128)(2,1)}, u32[]{:S(2)}) %copy-start.3) | copy-done | bytes 131096
  6.4 0.0 copy-start.4
  6.4 0.7 %copy-done.4 = f32[9,256]{1,0:T(8,128)S(1)} copy-done((f32[9,256]{1,0:T(8,128)S(1)}, f32[9,256]{1,0:T(8,128)}, u32[]{:S(2)}) %copy-start.4) | copy-done | bytes 9240
  7.1 0.0 copy-start.5
  7.1 0.7 %copy-done.5 = f32[256]{0:T(256)S(1)} copy-done((f32[256]{0:T(256)S(1)}, f32[256]{0:T(256)}, u32[]{:S(2)}) %copy-start.5) | copy-done | bytes 1048
  7.8 43.4 %shard_map.127 = (bf16[2560,256]{1,0:T(8,128)(2,1)S(1)}, f32[1024,256]{1,0:T(8,128)S(1)}, f32[1,256]{1,0:T(1,128)S(1)}, f32[9,256]{1,0:T(8,128)S(1)}, f32[256,256]{1,0:T(8,128)S(1)}, /*index=5*/f32[16,256]{1,0:T(8,128)S(1)}) custom-call(bf16[2560,256]{1,0:T(8,128)(2,1)S(1)} %bitcast.6, bf16[1024,256]{1,0:T(8,128)(2,1)S(1)} %copy-done.1, ...), custom_call_target="tpu_custom_call" | custom-call | tf_op jit(solution)/shard_map/pallas_call | solution.py:359
  51.2 0.6 %reshape.36 = f32[4,4,256]{2,1,0:T(4,128)} reshape(f32[16,256]{1,0:T(8,128)S(1)} %get-tuple-element.17) | data formatting | bytes 32768 | tf_op jit(solution)/shard_map/reshape | solution.py:422
  51.8 1.1 %copy.19 = bf16[1,2560,256]{2,1,0:T(8,128)(2,1)} copy(bf16[1,2560,256]{2,1,0:T(8,128)(2,1)S(1)} %bitcast.5) | data formatting | bytes 2621440
  52.8 1.0 %copy.20 = f32[1024,256]{1,0:T(8,128)} copy(f32[1024,256]{1,0:T(8,128)S(1)} %get-tuple-element.25) | data formatting | bytes 2097152
  53.8 0.6 %copy.21 = f32[256]{0:T(256)} copy(f32[256]{0:T(256)S(1)} %bitcast.8) | data formatting | bytes 2048
  54.4 0.6 %copy.22 = f32[9,256]{1,0:T(8,128)} copy(f32[9,256]{1,0:T(8,128)S(1)} %get-tuple-element.27) | data formatting | bytes 18432
  55.0 0.7 %copy.23 = f32[256,256]{1,0:T(8,128)} copy(f32[256,256]{1,0:T(8,128)S(1)} %get-tuple-element.28) | data formatting | bytes 524288
Async XLA Ops:
  2.1 1.3 %copy-start = (bf16[1,2560,256]{2,1,0:T(8,128)(2,1)S(1)}, bf16[1,2560,256]{2,1,0:T(8,128)(2,1)}, u32[]{:S(2)}) copy-start(bf16[1,2560,256]{2,1,0:T(8,128)(2,1)} %param.8) | copy-start | bytes 3932164
  3.4 1.0 %copy-start.1 = (bf16[1024,256]{1,0:T(8,128)(2,1)S(1)}, bf16[1024,256]{1,0:T(8,128)(2,1)}, u32[]{:S(2)}) copy-start(bf16[1024,256]{1,0:T(8,128)(2,1)} %weight.1) | copy-start | bytes 1572868
  4.5 1.0 %copy-start.2 = (bf16[4,160,256]{2,1,0:T(8,128)(2,1)S(1)}, bf16[4,160,256]{2,1,0:T(8,128)(2,1)}, u32[]{:S(2)}) copy-start(bf16[4,160,256]{2,1,0:T(8,128)(2,1)} %cot.1) | copy-start | bytes 983044
  5.5 0.9 %copy-start.3 = (bf16[256,256]{1,0:T(8,128)(2,1)S(1)}, bf16[256,256]{1,0:T(8,128)(2,1)}, u32[]{:S(2)}) copy-start(bf16[256,256]{1,0:T(8,128)(2,1)} %point.1) | copy-start | bytes 393220
  6.4 0.7 %copy-start.4 = (f32[9,256]{1,0:T(8,128)S(1)}, f32[9,256]{1,0:T(8,128)}, u32[]{:S(2)}) copy-start(f32[9,256]{1,0:T(8,128)} %taps.1) | copy-start | bytes 27652
  7.1 0.7 %copy-start.5 = (f32[256]{0:T(256)S(1)}, f32[256]{0:T(256)}, u32[]{:S(2)}) copy-start(f32[256]{0:T(256)} %param.10) | copy-start | bytes 3076

commit v3 on v2

--- a/solution.py
+++ b/solution.py
@@ -15,13 +15,14 @@
 
 
 def kernel(
-    rows, scale, act, weight, bias, taps, point, mix, perm, cot,
-    out_input, out_down, out_bias, out_taps, out_point, out_mix,
+    rows, act_in, weight_in, bias_in, taps_in, point_in, mix_in, maps_in, cot_in,
+    out_input, out_full,
+    act, weight, bias, taps, point, mix, maps, cot, perm, result,
     fine, rows_in, rows_t, preact, pooled, wide, gwide, grad, spread, mixed_low,
     mg_send, mg_recv, mix_send, mix_recv, edge, edge_send, edge_recv, back_send, back_recv, pre,
-    packed, core_in, half, parts, mine, gathered, other,
-    mg_sems, mix_sems, edge_sems, back_sems,
-    core_sems, part_send, part_recv, all_send, all_recv, pair_send, pair_recv,
+    packed, core_in, half, plane_in, line_out, line_in, full,
+    in_sems, out_sems, mg_sems, mix_sems, edge_sems, back_sems,
+    core_sems, plane_sems, line_sems, line_back, plane_send, plane_recv, pair_send, pair_recv,
 ):
     f32, low = jnp.float32, jnp.bfloat16
     tm, pix = lax.axis_index("tm"), lax.axis_index("pix")
@@ -29,6 +30,8 @@
     group = n_tm // 2 * n_pix
     core = lax.rem(tm, 2)
     me = tm // 2 * n_pix + pix
+    n_plane, n_line = n_tm // 2 * 2, n_pix // 2
+    mine, line = tm // 2 * 2 + lax.rem(pix, 2), pix // 2
     partner = (tm + 1 - 2 * core, pix)
     west, east = (tm, lax.rem(pix + n_pix - 1, n_pix)), (tm, lax.rem(pix + 1, n_pix))
     quarter = TR * TC // n_tm
@@ -36,6 +39,18 @@
     def peer(step):
         index = lax.rem(me + step, group)
         return index, (index // n_pix * 2 + core, lax.rem(index, n_pix))
+
+    loads = [
+        pltpu.make_async_copy(there, here, in_sems.at[i])
+        for i, (there, here) in enumerate(
+            [
+                (cot_in, cot), (mix_in, mix), (act_in, act), (weight_in, weight), (bias_in, bias),
+                (point_in, point), (taps_in, taps), (maps_in, maps),
+            ]
+        )
+    ]
+    for load in loads:
+        load.start()
 
     barrier = pltpu.get_barrier_semaphore()
     pl.semaphore_signal(barrier, inc=1, device_id=partner, device_id_type=MESH)
@@ -47,12 +62,12 @@
         _, device = peer(step)
         pl.semaphore_signal(barrier, inc=1, device_id=device, device_id_type=MESH)
 
+    loads[0].wait()
+    loads[1].wait()
     for frame in range(n_tm):
-        total = mix[frame : frame + 1] * cot[0].astype(f32)
+        total = mix[0, frame : frame + 1] * cot[0].astype(f32)
         for source in range(1, n_tm):
-            total = total + mix[n_tm * source + frame : n_tm * source + frame + 1] * cot[
-                source
-            ].astype(f32)
+            total = total + mix[source, frame : frame + 1] * cot[source].astype(f32)
         mg_send[frame] = total.astype(low)
     pl.semaphore_wait(barrier, group + 1)
 
@@ -65,6 +80,13 @@
     for step in range(1, n_tm):
         exchange(mg_send, mg_recv, mg_sems, step).start()
     mg_recv[tm] = mg_send[tm]
+
+    for load in loads[2:]:
+        load.wait()
+    perm[...] = jnp.zeros(perm.shape, f32)
+    for side in range(2):
+        row = lax.broadcasted_iota(jnp.int32, (TR, TR), 0)
+        perm[side, 0:TR, 0:TR] = jnp.where(maps[0, side : side + 1, :] == row, 1.0, 0.0)
 
     @pl.loop(0, 2560 // 160)
     def _(i):
@@ -148,7 +170,7 @@
             tap = 3 * a + 2 * side
             total = total + taps[tap : tap + 1] * edge[side, 2 - a : 2 - a + TR]
         total = jnp.concatenate([total, jnp.zeros((32 - TR, C), f32)], axis=0).astype(low)
-        back_send[side] = jnp.dot(perm[side], total, preferred_element_type=f32).astype(low)
+        back_send[side] = jnp.dot(perm[side].astype(low), total, preferred_element_type=f32).astype(low)
     backward = swap_edges(back_send, back_recv, back_sems)
     for copy in backward:
         copy.start()
@@ -156,7 +178,7 @@
     for copy in forward:
         copy.wait()
     for side in range(2):
-        edge[side] = jnp.dot(perm[side], edge_recv[side], preferred_element_type=f32)
+        edge[side] = jnp.dot(perm[side].astype(low), edge_recv[side], preferred_element_type=f32)
     for r in range(TR):
         wide[0, r + 1, 0:1, :] = edge[0, r : r + 1]
         wide[2, r + 1, TC - 1 : TC, :] = edge[1, r : r + 1]
@@ -252,25 +274,48 @@
     for side in range(2):
         packed[side, 1312:, :] = jnp.zeros((group * rows - 1312, 128), low)
 
-    swap = pltpu.make_async_remote_copy(
-        packed.at[1 - core], core_in, core_sems.at[0], core_sems.at[1], partner, MESH
-    )
-    swap.start()
-    swap.wait()
-    half[...] = (packed[core].astype(f32) + core_in[...].astype(f32)).astype(low)
-
-    def send_part(step):
-        index, device = peer(step)
-        return pltpu.make_async_remote_copy(
-            half.at[pl.ds(pl.multiple_of(index * rows, 16), rows)],
-            parts.at[step], part_send.at[step], part_recv.at[step], device, MESH
-        )
-
-    @pl.loop(1, group)
-    def _(step):
-        send_part(step).start()
-
-    parts[0] = half[pl.ds(pl.multiple_of(me * rows, 16), rows), :]
+    span = n_line * rows
+
+    def plane_peer(step):
+        index = lax.rem(mine + step, n_plane)
+        return index, (index // 2 * 2 + core, line * 2 + lax.rem(index, 2))
+
+    def line_peer(step):
+        index = lax.rem(line + step, n_line)
+        return index, (tm, index * 2 + lax.rem(pix, 2))
+
+    def span_of(step):
+        index, _ = plane_peer(step)
+        return pl.ds(pl.multiple_of(index * span, 16), span)
+
+    def swap(step):
+        return pltpu.make_async_remote_copy(
+            packed.at[1 - core, span_of(step)], core_in.at[span_of(step)],
+            core_sems.at[0, step], core_sems.at[1, step], partner, MESH
+        )
+
+    def to_plane(step):
+        return pltpu.make_async_remote_copy(
+            half.at[span_of(step)], plane_in.at[step],
+            plane_sems.at[0, step], plane_sems.at[1, step], plane_peer(step)[1], MESH
+        )
+
+    def to_line(step):
+        index, device = line_peer(step)
+        return pltpu.make_async_remote_copy(
+            line_out.at[index], line_in.at[step],
+            line_sems.at[0, step], line_sems.at[1, step], device, MESH
+        )
+
+    order = list(range(1, n_plane)) + [0]
+    for step in order:
+        swap(step).start()
+    for step in order:
+        swap(step).wait()
+        at = span_of(step)
+        half[at, :] = (packed[core, at, :].astype(f32) + core_in[at, :].astype(f32)).astype(low)
+        if step:
+            to_plane(step).start()
 
     for child in range(4):
         lanes = slice(child * C, child * C + C)
@@ -280,63 +325,132 @@
         for side in range(2):
             fine[side, pl.ds(child, TR * TC, stride=4), :] = value[:, side * 128 : side * 128 + 128]
 
+    for step in range(1, n_plane):
+        to_plane(step).wait()
+
+    def line_sum(step):
+        index, _ = line_peer(step)
+        at = pl.ds(pl.multiple_of(mine * span + index * rows, 16), rows)
+        total = half[at, :].astype(f32)
+        for other in range(1, n_plane):
+            total = total + plane_in[
+                other, pl.ds(pl.multiple_of(index * rows, 16), rows), :
+            ].astype(f32)
+        line_out[index] = total.astype(low)
+
+    @pl.loop(1, n_line)
+    def _(step):
+        line_sum(step)
+        to_line(step).start()
+
+    line_sum(0)
+
     @pl.loop(0, 2560 // 160)
     def _(i):
         at = pl.ds(pl.multiple_of(i * 160, 160), 160)
         for side in range(2):
-            out_input[at, side * 128 : side * 128 + 128] = fine[side, at, :].astype(low)
-
-    @pl.loop(1, group)
-    def _(step):
-        send_part(step).wait()
+            result[at, side * 128 : side * 128 + 128] = fine[side, at, :].astype(low)
+
+    store = pltpu.make_async_copy(result, out_input, out_sems.at[0])
+    store.start()
+
+    @pl.loop(1, n_line)
+    def _(step):
+        to_line(step).wait()
 
     def add(step, total):
-        return total + parts[step].astype(f32)
-
-    mine[...] = lax.fori_loop(0, group, add, jnp.zeros((rows, 128), f32)).astype(low)
-
-    def send_all(step):
-        _, device = peer(step)
-        return pltpu.make_async_remote_copy(
-            mine, gathered.at[step], all_send.at[step], all_recv.at[step], device, MESH
-        )
-
-    def send_pair(step):
-        return pltpu.make_async_remote_copy(
-            gathered.at[step], other.at[step], pair_send.at[step], pair_recv.at[step], partner, MESH
-        )
-
-    @pl.loop(1, group)
-    def _(step):
-        send_all(step).start()
-
-    gathered[0] = mine[...]
-    send_pair(0).start()
-
-    @pl.loop(1, group)
-    def _(step):
-        send_all(step).wait()
-        send_pair(step).start()
-
-    @pl.loop(0, group)
-    def _(step):
-        send_pair(step).wait()
-
-    @pl.loop(0, group)
-    def _(step):
-        index = lax.rem(me + group - step, group)
-        place = pl.ds(pl.multiple_of(index * rows, 16), rows)
-        packed[core, place, :] = gathered[step]
-        packed[1 - core, place, :] = other[step]
-
+        return total + line_in[step].astype(f32)
+
+    def place(plane_step, line_step):
+        index = lax.rem(mine + n_plane - plane_step, n_plane) * n_line + lax.rem(
+            line + n_line - line_step, n_line
+        )
+        return full.at[core, pl.ds(pl.multiple_of(index * rows, 16), rows)]
+
+    first = pl.ds(pl.multiple_of((mine * n_line + line) * rows, 16), rows)
+    full[core, first, :] = lax.fori_loop(1, n_line, add, line_out[line].astype(f32)).astype(low)
+
+    def back_line(step):
+        return pltpu.make_async_remote_copy(
+            place(0, 0), place(0, 0),
+            line_back.at[0, step], line_back.at[1, step], line_peer(step)[1], MESH
+        )
+
+    def back_plane(plane_step, step):
+        return pltpu.make_async_remote_copy(
+            place(0, step), place(0, step), plane_send.at[plane_step, step],
+            plane_recv.at[plane_step, step], plane_peer(plane_step)[1], MESH
+        )
+
+    def back_pair(plane_step, step):
+        return pltpu.make_async_remote_copy(
+            place(plane_step, step), place(plane_step, step), pair_send.at[plane_step, step],
+            pair_recv.at[plane_step, step], partner, MESH
+        )
+
+    @pl.loop(1, n_line)
+    def _(step):
+        back_line(step).start()
+
+    for plane_step in range(1, n_plane):
+        back_plane(plane_step, 0).start()
+    back_pair(0, 0).start()
+
+    @pl.loop(1, n_line)
+    def _(step):
+        back_line(step).wait()
+        for plane_step in range(1, n_plane):
+            back_plane(plane_step, step).start()
+        back_pair(0, step).start()
+
+    @pl.loop(0, n_line)
+    def _(step):
+        for plane_step in range(1, n_plane):
+            back_plane(plane_step, step).wait()
+            back_pair(plane_step, step).start()
+
+    @pl.loop(0, n_line)
+    def _(step):
+        for plane_step in range(n_plane):
+            back_pair(plane_step, step).wait()
+
+    store_full = pltpu.make_async_copy(full, out_full, out_sems.at[1])
+    store_full.start()
+    store.wait()
+    store_full.wait()
+
+
+def unpack_kernel(
+    scale, fine_in, full_in, out_input, out_down, out_bias, out_taps, out_point, out_mix,
+    full, down, bias, taps, point, mix, sems,
+):
+    f32 = jnp.float32
+    through = pltpu.make_async_copy(fine_in, out_input, sems.at[0])
+    through.start()
+    load = pltpu.make_async_copy(full_in, full, sems.at[1])
+    load.start()
+    load.wait()
     for side in range(2):
         lanes = slice(side * 128, side * 128 + 128)
-        out_down[:, lanes] = packed[side, 0:1024, :].astype(f32) * scale
-        out_point[:, lanes] = packed[side, 1024:1280, :].astype(f32) * scale
-        tail = packed[side, 1280:1312, :].astype(f32) * scale
-        out_taps[:, lanes] = tail[0:9]
-        out_mix[:, lanes] = tail[9:25]
-        out_bias[:, lanes] = tail[25:26]
+        tail = full[side, 5 * C : 5 * C + 32, :].astype(f32) * scale
+        taps[:, lanes] = tail[0:9]
+        for frame in range(mix.shape[0]):
+            first = 9 + frame * mix.shape[1]
+            mix[frame, :, lanes] = tail[first : first + mix.shape[1]]
+        bias[lanes] = tail[25]
+        point[:, lanes] = full[side, 4 * C : 5 * C, :].astype(f32) * scale
+        down[:, lanes] = full[side, 0 : 4 * C, :].astype(f32) * scale
+    stores = [
+        pltpu.make_async_copy(here, there, sems.at[2 + i])
+        for i, (here, there) in enumerate(
+            [(down, out_down), (bias, out_bias), (taps, out_taps), (point, out_point), (mix, out_mix)]
+        )
+    ]
+    for store in stores:
+        store.start()
+    for store in stores:
+        store.wait()
+    through.wait()
 
 
 def on_device(
@@ -350,25 +464,29 @@
     group = frames // 2 * tiles
     rows = -(-1312 // (16 * group)) * 16
     f32, low = jnp.float32, jnp.bfloat16
-    sems = pltpu.SemaphoreType.DMA((group,))
     both = lambda n: pltpu.SemaphoreType.DMA((2, n))
-    place = lax.broadcasted_iota(jnp.int32, (2, 32, 32), 2)
-    maps = jnp.pad(edge_rows[0], ((0, 0), (0, 32 - TR)), constant_values=-1)
-    perm = (maps[:, :, None] == place).astype(low)
-    vmem = pl.BlockSpec(memory_space=pltpu.VMEM)
-    outs = pl.pallas_call(
-        functools.partial(kernel, rows, scale),
+    n_plane, n_line = frames // 2 * 2, tiles // 2
+    grid = pltpu.SemaphoreType.DMA((n_plane, n_line))
+    hbm = pl.BlockSpec(memory_space=pltpu.HBM)
+    fine, full = pl.pallas_call(
+        functools.partial(kernel, rows),
         out_shape=[
             jax.ShapeDtypeStruct((4 * pixels, C), low),
-            jax.ShapeDtypeStruct((4 * C, C), f32),
-            jax.ShapeDtypeStruct((1, C), f32),
-            jax.ShapeDtypeStruct((9, C), f32),
-            jax.ShapeDtypeStruct((C, C), f32),
-            jax.ShapeDtypeStruct((frames * frames, C), f32),
+            jax.ShapeDtypeStruct((2, group * rows, 128), low),
         ],
-        in_specs=[vmem] * 8,
-        out_specs=[vmem] * 6,
+        in_specs=[hbm] * 8,
+        out_specs=[hbm] * 2,
         scratch_shapes=[
+            pltpu.VMEM((4 * pixels, C), low),
+            pltpu.VMEM((4 * C, C), low),
+            pltpu.VMEM((1, C), f32),
+            pltpu.VMEM((9, C), f32),
+            pltpu.VMEM((C, C), low),
+            pltpu.VMEM((frames, frames, C), f32),
+            pltpu.VMEM((1, 2, TR), jnp.int32),
+            pltpu.VMEM((frames, quarter, C), low),
+            pltpu.VMEM((2, 32, 32), f32),
+            pltpu.VMEM((4 * pixels, C), low),
             pltpu.VMEM((2, 4 * pixels, 128), f32),
             pltpu.VMEM((pixels, 4 * C), low),
             pltpu.VMEM((4 * C, pixels), low),
@@ -392,13 +510,14 @@
             pltpu.VMEM((2, group * rows, 128), low),
             pltpu.VMEM((group * rows, 128), low),
             pltpu.VMEM((group * rows, 128), low),
-            pltpu.VMEM((group, rows, 128), low),
-            pltpu.VMEM((rows, 128), low),
-            pltpu.VMEM((group, rows, 128), low),
-            pltpu.VMEM((group, rows, 128), low),
+            pltpu.VMEM((n_plane, n_line * rows, 128), low),
+            pltpu.VMEM((n_line, rows, 128), low),
+            pltpu.VMEM((n_line, rows, 128), low),
+            pltpu.VMEM((2, group * rows, 128), low),
+            pltpu.SemaphoreType.DMA((8,)),
+            pltpu.SemaphoreType.DMA((2,)),
             both(frames), both(frames), both(2), both(2),
-            pltpu.SemaphoreType.DMA((2,)),
-            sems, sems, sems, sems, sems, sems,
+            both(n_plane), both(n_plane), both(n_line), both(n_line), grid, grid, grid, grid,
         ],
         compiler_params=pltpu.CompilerParams(
             collective_id=0, has_side_effects=True, vmem_limit_bytes=48 * 1024 * 1024
@@ -409,18 +528,23 @@
         down_bias.reshape(1, C),
         taps,
         point_weight,
-        time_mix.reshape(frames * frames, C),
-        perm,
+        time_mix,
+        edge_rows,
         cotangent,
     )
-    return (
-        outs[0].reshape(1, 4 * pixels, C),
-        outs[1],
-        outs[2].reshape(C),
-        outs[3],
-        outs[4],
-        outs[5].reshape(frames, frames, C),
-    )
+    shapes = [(4 * C, C), (C,), (9, C), (C, C), (frames, frames, C)]
+    outs = pl.pallas_call(
+        functools.partial(unpack_kernel, scale),
+        out_shape=[jax.ShapeDtypeStruct((4 * pixels, C), low)]
+        + [jax.ShapeDtypeStruct(shape, f32) for shape in shapes],
+        in_specs=[hbm] * 2,
+        out_specs=[hbm] * 6,
+        scratch_shapes=[pltpu.VMEM((2, group * rows, 128), low)]
+        + [pltpu.VMEM(shape, f32) for shape in shapes]
+        + [pltpu.SemaphoreType.DMA((7,))],
+        compiler_params=pltpu.CompilerParams(vmem_limit_bytes=32 * 1024 * 1024),
+    )(fine, full)
+    return (outs[0].reshape(1, 4 * pixels, C), *outs[1:])
 
 
 def solution(mesh):

time: 56.1 us -> 53.1 us (0.947)
  local copies, waits for them, and re-layouts: 11.6 us -> 7.02 us
  Pallas kernels: 43.4 us -> 45 us
    unnamed x17 -> x16, local copies, waits for them, and re-layouts: 9.52 us -> 7.02 us
    pallas_call x1 -> x2, Pallas kernels: 43.4 us -> 45 us  [the longest x1 43.4 us: on_device(): pl.pallas_call(functools.partial(kernel, rows), out_shape=[jax.ShapeDtype...]
    reshape x2 -> x0, local copies, waits for them, and re-layouts: 1.35 us -> none  [the longest x1 0.73 us: on_device(): time_mix.reshape(frames * frames, C)]
    pad x1 -> x0, local copies, waits for them, and re-layouts: 0.69 us -> none  [on_device(): maps = jnp.pad(edge_rows[0], ((0, 0), (0, 32 - TR)), constant_values=-1)]
where the time goes in v3:
time: 53.1 us; the launch traced here: 52.7 us
  Pallas kernels  45 us (85%)
  local copies, waits for them, and re-layouts  7.02 us (13%)
  between operations  0.66 us (1%)
    pallas_call x1, Pallas kernels, on_device(): pl.pallas_call(functools.partial(kernel, rows), out_shape=[jax.ShapeDtype...  43.4 us
    unnamed x16, local copies, waits for them, and re-layouts  7.02 us
    pallas_call x1, Pallas kernels, on_device(): pl.pallas_call(functools.partial(unpack_kernel, scale), out_shape=[jax.Sh...  1.56 us

profile of v3, /device:TPU:0, one launch (start us, length us, event | category | flops | bytes accessed | tf_op | source)
XLA Modules:
  0.0 52.7 jit_solution(95897960417536393)
XLA Ops:
  0.6 0.0 copy-start
  0.6 1.3 %copy-done = bf16[1,2560,256]{2,1,0:T(8,128)(2,1)S(1)} copy-done((bf16[1,2560,256]{2,1,0:T(8,128)(2,1)S(1)}, bf16[1,2560,256]{2,1,0:T(8,128)(2,1)}, u32[]{:S(2)}) %copy-start) | copy-done | bytes 1310744
  2.0 0.0 copy-start.1
  2.0 1.0 %copy-done.1 = bf16[1024,256]{1,0:T(8,128)(2,1)S(1)} copy-done((bf16[1024,256]{1,0:T(8,128)(2,1)S(1)}, bf16[1024,256]{1,0:T(8,128)(2,1)}, u32[]{:S(2)}) %copy-start.1) | copy-done | bytes 524312
  3.0 0.0 copy-start.2
  3.0 1.0 %copy-done.2 = bf16[4,160,256]{2,1,0:T(8,128)(2,1)S(1)} copy-done((bf16[4,160,256]{2,1,0:T(8,128)(2,1)S(1)}, bf16[4,160,256]{2,1,0:T(8,128)(2,1)}, u32[]{:S(2)}) %copy-start.2) | copy-done | bytes 327704
  4.0 0.0 copy-start.3
  4.0 0.9 %copy-done.3 = bf16[256,256]{1,0:T(8,128)(2,1)S(1)} copy-done((bf16[256,256]{1,0:T(8,128)(2,1)S(1)}, bf16[256,256]{1,0:T(8,128)(2,1)}, u32[]{:S(2)}) %copy-start.3) | copy-done | bytes 131096
  4.9 0.0 copy-start.4
  4.9 0.7 %copy-done.4 = f32[9,256]{1,0:T(8,128)S(1)} copy-done((f32[9,256]{1,0:T(8,128)S(1)}, f32[9,256]{1,0:T(8,128)}, u32[]{:S(2)}) %copy-start.4) | copy-done | bytes 9240
  5.6 0.0 copy-start.5
  5.6 0.7 %copy-done.5 = f32[4,4,256]{2,1,0:T(4,128)S(1)} copy-done((f32[4,4,256]{2,1,0:T(4,128)S(1)}, f32[4,4,256]{2,1,0:T(4,128)}, u32[]{:S(2)}) %copy-start.5) | copy-done | bytes 16408
  6.3 0.0 copy-start.6
  6.3 0.7 %copy-done.6 = f32[256]{0:T(256)S(1)} copy-done((f32[256]{0:T(256)S(1)}, f32[256]{0:T(256)}, u32[]{:S(2)}) %copy-start.6) | copy-done | bytes 1048
  7.0 0.0 copy-start.7
  7.0 0.7 %copy-done.7 = s32[1,2,20]{2,1,0:T(2,128)S(1)} copy-done((s32[1,2,20]{2,1,0:T(2,128)S(1)}, s32[1,2,20]{2,1,0:T(2,128)}, u32[]{:S(2)}) %copy-start.7) | copy-done | bytes 184
  7.7 43.4 %shard_map.127 = (bf16[2560,256]{1,0:T(8,128)(2,1)S(1)}, bf16[2,1536,128]{2,1,0:T(8,128)(2,1)S(1)}) custom-call(bf16[2560,256]{1,0:T(8,128)(2,1)S(1)} %bitcast.3, bf16[1024,256]{1,0:T(8,128)(2,1)S(1)} %copy-done.1, f32[1,256]{1,0:T(1,128)S(1)} %bitcast.4, f32[9,256]{1,0:T(8,128)S(1)} %copy-done.4, bf16[256,256]{1,0:T(8,128)(2,1)S(1)} %copy-done.3, ...), custom_call_target="tpu_custom_call" | custom-call | tf_op jit(solution)/shard_map/pallas_call | solution.py:471
  51.1 1.6 %shard_map.128 = (bf16[2560,256]{1,0:T(8,128)(2,1)}, f32[1024,256]{1,0:T(8,128)}, f32[256]{0:T(256)}, f32[9,256]{1,0:T(8,128)}, f32[256,256]{1,0:T(8,128)}, /*index=5*/f32[4,4,256]{2,1,0:T(4,128)}) custom-call(bf16[2560,256]{1,0:T(8,128)(2,1)S(1)} %get-tuple-element.14.fine_in, bf16[2,1536,128]{2,1,0:T(8,128)(2,1)S(1)} %get-tuple-element.15.full_in), custom_call_target="tpu_custom_call" | custom-call | tf_op jit(solution)/shard_map/pallas_call | solution.py:536
Async XLA Ops:
  0.6 1.3 %copy-start = (bf16[1,2560,256]{2,1,0:T(8,128)(2,1)S(1)}, bf16[1,2560,256]{2,1,0:T(8,128)(2,1)}, u32[]{:S(2)}) copy-start(bf16[1,2560,256]{2,1,0:T(8,128)(2,1)} %param.8) | copy-start | bytes 3932164
  2.0 1.0 %copy-start.1 = (bf16[1024,256]{1,0:T(8,128)(2,1)S(1)}, bf16[1024,256]{1,0:T(8,128)(2,1)}, u32[]{:S(2)}) copy-start(bf16[1024,256]{1,0:T(8,128)(2,1)} %weight_in.1) | copy-start | bytes 1572868
  3.0 1.0 %copy-start.2 = (bf16[4,160,256]{2,1,0:T(8,128)(2,1)S(1)}, bf16[4,160,256]{2,1,0:T(8,128)(2,1)}, u32[]{:S(2)}) copy-start(bf16[4,160,256]{2,1,0:T(8,128)(2,1)} %cot_in.1) | copy-start | bytes 983044
  4.0 0.9 %copy-start.3 = (bf16[256,256]{1,0:T(8,128)(2,1)S(1)}, bf16[256,256]{1,0:T(8,128)(2,1)}, u32[]{:S(2)}) copy-start(bf16[256,256]{1,0:T(8,128)(2,1)} %point_in.1) | copy-start | bytes 393220
  4.9 0.7 %copy-start.4 = (f32[9,256]{1,0:T(8,128)S(1)}, f32[9,256]{1,0:T(8,128)}, u32[]{:S(2)}) copy-start(f32[9,256]{1,0:T(8,128)} %taps_in.1) | copy-start | bytes 27652
  5.6 0.7 %copy-start.5 = (f32[4,4,256]{2,1,0:T(4,128)S(1)}, f32[4,4,256]{2,1,0:T(4,128)}, u32[]{:S(2)}) copy-start(f32[4,4,256]{2,1,0:T(4,128)} %mix_in.1) | copy-start | bytes 49156
  6.3 0.7 %copy-start.6 = (f32[256]{0:T(256)S(1)}, f32[256]{0:T(256)}, u32[]{:S(2)}) copy-start(f32[256]{0:T(256)} %param.10) | copy-start | bytes 3076
  7.0 0.7 %copy-start.7 = (s32[1,2,20]{2,1,0:T(2,128)S(1)}, s32[1,2,20]{2,1,0:T(2,128)}, u32[]{:S(2)}) copy-start(s32[1,2,20]{2,1,0:T(2,128)} %maps_in.1) | copy-start | bytes 484

commit v4 on v3

--- a/solution.py
+++ b/solution.py
@@ -15,14 +15,14 @@
 
 
 def kernel(
-    rows, act_in, weight_in, bias_in, taps_in, point_in, mix_in, maps_in, cot_in,
+    rows, rest_rows, act_in, weight_in, bias_in, taps_in, point_in, mix_in, maps_in, cot_in,
     out_input, out_full,
     act, weight, bias, taps, point, mix, maps, cot, perm, result,
     fine, rows_in, rows_t, preact, pooled, wide, gwide, grad, spread, mixed_low,
     mg_send, mg_recv, mix_send, mix_recv, edge, edge_send, edge_recv, back_send, back_recv, pre,
-    packed, core_in, half, plane_in, line_out, line_in, full,
+    packed, core_in, half, full, plane_in, line_out, line_in, rest_plane_in, rest_line_out, rest_line_in,
     in_sems, out_sems, mg_sems, mix_sems, edge_sems, back_sems,
-    core_sems, plane_sems, line_sems, line_back, plane_send, plane_recv, pair_send, pair_recv,
+    *total_sems,
 ):
     f32, low = jnp.float32, jnp.bfloat16
     tm, pix = lax.axis_index("tm"), lax.axis_index("pix")
@@ -175,60 +175,23 @@
     for copy in backward:
         copy.start()
 
-    for copy in forward:
-        copy.wait()
-    for side in range(2):
-        edge[side] = jnp.dot(perm[side].astype(low), edge_recv[side], preferred_element_type=f32)
-    for r in range(TR):
-        wide[0, r + 1, 0:1, :] = edge[0, r : r + 1]
-        wide[2, r + 1, TC - 1 : TC, :] = edge[1, r : r + 1]
-
-    def conv(r, sums):
-        total = jnp.zeros((TC, C), f32)
-        inner = mg_recv[r // (TR // n_tm), pl.ds(
-            pl.multiple_of(lax.rem(r, TR // n_tm) * TC, TC), TC
-        ), :].astype(f32)
-        here = gwide[1, r + 1]
-        new = []
-        for a in range(3):
-            for b in range(3):
-                tap = taps[3 * a + b : 3 * a + b + 1]
-                cells = wide[b, r + a]
-                total = total + tap * cells
-                inner = inner + tap * gwide[2 - b, r + 2 - a]
-                product = here * cells
-                new.append(
-                    sums[3 * a + b]
-                    + ((product[0:8] + product[8:16]) + (product[16:24] + product[24:32]))
-                )
-        at = pl.ds(pl.multiple_of(r * TC, TC), TC)
-        spread[at, :] = total.astype(low)
-        grad[at, :] = inner
-        return tuple(new)
-
-    sums = lax.fori_loop(0, TR, conv, tuple(jnp.zeros((8, C), f32) for _ in range(9)))
-    taps_part = [jnp.sum(x, axis=0, keepdims=True) for x in sums]
-
-    @pl.loop(0, n_tm)
-    def _(i):
-        at = pl.ds(pl.multiple_of(i * quarter, quarter), quarter)
-        value = jnp.dot(spread[at, :], point[...], preferred_element_type=f32)
-        mix_send[i] = (pooled[at, :].astype(f32) + value).astype(low)
-        mixed_low[at, :] = mg_recv[i]
-
-    for step in range(1, n_tm):
-        exchange(mix_send, mix_recv, mix_sems, step).start()
-    mix_recv[tm] = mix_send[tm]
-
     def pack(first, value):
         for side in range(2):
             packed[side, first : first + value.shape[0], :] = value[
                 :, side * 128 : side * 128 + 128
             ].astype(low)
 
-    across_rows = (((0,), (0,)), ((), ()))
-    pack(4 * C, lax.dot_general(spread[...], mixed_low[...], across_rows, preferred_element_type=f32))
-
+    def inner(r, carry):
+        value = mg_recv[r // (TR // n_tm), pl.ds(
+            pl.multiple_of(lax.rem(r, TR // n_tm) * TC, TC), TC
+        ), :].astype(f32)
+        for a in range(3):
+            for b in range(3):
+                value = value + taps[3 * a + b : 3 * a + b + 1] * gwide[2 - b, r + 2 - a]
+        grad[pl.ds(pl.multiple_of(r * TC, TC), TC), :] = value
+        return carry
+
+    lax.fori_loop(0, TR, inner, 0)
     for copy in backward:
         copy.wait()
     edge[...] = back_recv[...].astype(f32)
@@ -249,6 +212,200 @@
     for child in range(4):
         lanes = slice(child * C, child * C + C)
         pack(child * C, jnp.dot(rows_t[lanes, :], pre[...], preferred_element_type=f32))
+    size = group * rows
+    for side in range(2):
+        if size > 4 * C:
+            packed[side, 4 * C : size, :] = jnp.zeros((size - 4 * C, 128), low)
+
+    def plane_peer(step):
+        index = lax.rem(mine + step, n_plane)
+        return index, (index // 2 * 2 + core, line * 2 + lax.rem(index, 2))
+
+    def line_peer(step):
+        index = lax.rem(line + step, n_line)
+        return index, (tm, index * 2 + lax.rem(pix, 2))
+
+    def total_stages(base, rows, plane_in, line_out, line_in, sems):
+        core_sems, plane_sems, line_sems, line_back, plane_send, plane_recv, pair_send, pair_recv = sems
+        span = n_line * rows
+        order = list(range(1, n_plane)) + [0]
+
+        def span_of(step):
+            return pl.ds(pl.multiple_of(base + plane_peer(step)[0] * span, 16), span)
+
+        def swap(step):
+            return pltpu.make_async_remote_copy(
+                packed.at[1 - core, span_of(step)], core_in.at[span_of(step)],
+                core_sems.at[0, step], core_sems.at[1, step], partner, MESH
+            )
+
+        def to_plane(step):
+            return pltpu.make_async_remote_copy(
+                half.at[span_of(step)], plane_in.at[step],
+                plane_sems.at[0, step], plane_sems.at[1, step], plane_peer(step)[1], MESH
+            )
+
+        def to_line(step):
+            index, device = line_peer(step)
+            return pltpu.make_async_remote_copy(
+                line_out.at[index], line_in.at[step],
+                line_sems.at[0, step], line_sems.at[1, step], device, MESH
+            )
+
+        def place(plane_step, line_step):
+            index = lax.rem(mine + n_plane - plane_step, n_plane) * n_line + lax.rem(
+                line + n_line - line_step, n_line
+            )
+            return full.at[core, pl.ds(pl.multiple_of(base + index * rows, 16), rows)]
+
+        def back_line(step):
+            return pltpu.make_async_remote_copy(
+                place(0, 0), place(0, 0),
+                line_back.at[0, step], line_back.at[1, step], line_peer(step)[1], MESH
+            )
+
+        def back_plane(plane_step, step):
+            return pltpu.make_async_remote_copy(
+                place(0, step), place(0, step), plane_send.at[plane_step, step],
+                plane_recv.at[plane_step, step], plane_peer(plane_step)[1], MESH
+            )
+
+        def back_pair(plane_step, step):
+            return pltpu.make_async_remote_copy(
+                place(plane_step, step), place(plane_step, step), pair_send.at[plane_step, step],
+                pair_recv.at[plane_step, step], partner, MESH
+            )
+
+        def start():
+            for step in order:
+                swap(step).start()
+
+        def enter_plane():
+            for step in order:
+                swap(step).wait()
+                at = span_of(step)
+                half[at, :] = (packed[core, at, :].astype(f32) + core_in[at, :].astype(f32)).astype(
+                    low
+                )
+                if step:
+                    to_plane(step).start()
+
+        def enter_line():
+            for step in range(1, n_plane):
+                to_plane(step).wait()
+
+            def line_sum(step):
+                index, _ = line_peer(step)
+                at = pl.ds(pl.multiple_of(base + mine * span + index * rows, 16), rows)
+                total = half[at, :].astype(f32)
+                for other in range(1, n_plane):
+                    total = total + plane_in[
+                        other, pl.ds(pl.multiple_of(index * rows, 16), rows), :
+                    ].astype(f32)
+                line_out[index] = total.astype(low)
+
+            @pl.loop(1, n_line)
+            def _(step):
+                line_sum(step)
+                to_line(step).start()
+
+            line_sum(0)
+
+        def turn():
+            @pl.loop(1, n_line)
+            def _(step):
+                to_line(step).wait()
+
+            def add(step, total):
+                return total + line_in[step].astype(f32)
+
+            first = pl.ds(pl.multiple_of(base + (mine * n_line + line) * rows, 16), rows)
+            full[core, first, :] = lax.fori_loop(
+                1, n_line, add, line_out[line].astype(f32)
+            ).astype(low)
+
+            @pl.loop(1, n_line)
+            def _(step):
+                back_line(step).start()
+
+            for plane_step in range(1, n_plane):
+                back_plane(plane_step, 0).start()
+            back_pair(0, 0).start()
+
+        def leave_line():
+            @pl.loop(1, n_line)
+            def _(step):
+                back_line(step).wait()
+                for plane_step in range(1, n_plane):
+                    back_plane(plane_step, step).start()
+                back_pair(0, step).start()
+
+        def leave_plane():
+            @pl.loop(0, n_line)
+            def _(step):
+                for plane_step in range(1, n_plane):
+                    back_plane(plane_step, step).wait()
+                    back_pair(plane_step, step).start()
+
+        def finish():
+            @pl.loop(0, n_line)
+            def _(step):
+                for plane_step in range(n_plane):
+                    back_pair(plane_step, step).wait()
+
+        return start, enter_plane, enter_line, turn, leave_line, leave_plane, finish
+
+    down = total_stages(0, rows, plane_in, line_out, line_in, total_sems[:8])
+    rest = total_stages(
+        size, rest_rows, rest_plane_in, rest_line_out, rest_line_in, total_sems[8:]
+    )
+    down[0]()
+
+    for copy in forward:
+        copy.wait()
+    for side in range(2):
+        edge[side] = jnp.dot(
+            perm[side].astype(low), edge_recv[side], preferred_element_type=f32
+        )
+    for r in range(TR):
+        wide[0, r + 1, 0:1, :] = edge[0, r : r + 1]
+        wide[2, r + 1, TC - 1 : TC, :] = edge[1, r : r + 1]
+    down[1]()
+
+    def conv(r, sums):
+        total = jnp.zeros((TC, C), f32)
+        here = gwide[1, r + 1]
+        new = []
+        for a in range(3):
+            for b in range(3):
+                cells = wide[b, r + a]
+                total = total + taps[3 * a + b : 3 * a + b + 1] * cells
+                product = here * cells
+                new.append(
+                    sums[3 * a + b]
+                    + ((product[0:8] + product[8:16]) + (product[16:24] + product[24:32]))
+                )
+        spread[pl.ds(pl.multiple_of(r * TC, TC), TC), :] = total.astype(low)
+        return tuple(new)
+
+    sums = lax.fori_loop(0, TR, conv, tuple(jnp.zeros((8, C), f32) for _ in range(9)))
+    small = [jnp.sum(x, axis=0, keepdims=True) for x in sums]
+
+    @pl.loop(0, n_tm)
+    def _(i):
+        at = pl.ds(pl.multiple_of(i * quarter, quarter), quarter)
+        value = jnp.dot(spread[at, :], point[...], preferred_element_type=f32)
+        mix_send[i] = (pooled[at, :].astype(f32) + value).astype(low)
+        mixed_low[at, :] = mg_recv[i]
+
+    for step in range(1, n_tm):
+        exchange(mix_send, mix_recv, mix_sems, step).start()
+    mix_recv[tm] = mix_send[tm]
+    down[2]()
+
+    across_rows = (((0,), (0,)), ((), ()))
+    pack(size, lax.dot_general(spread[...], mixed_low[...], across_rows, preferred_element_type=f32))
+    down[3]()
 
     for step in range(1, n_tm):
         exchange(mix_send, mix_recv, mix_sems, step).wait()
@@ -267,55 +424,14 @@
     sums = lax.fori_loop(
         0, quarter // 16, mixing, tuple(jnp.zeros((8, C), f32) for _ in range(n_tm * n_tm))
     )
-    small = taps_part + [jnp.sum(x, axis=0, keepdims=True) for x in sums]
+    small += [jnp.sum(x, axis=0, keepdims=True) for x in sums]
     small.append(jnp.sum(bias_part, axis=0, keepdims=True))
     small.append(jnp.zeros((6, C), f32))
-    pack(5 * C, jnp.concatenate(small, axis=0))
+    pack(size + C, jnp.concatenate(small, axis=0))
     for side in range(2):
-        packed[side, 1312:, :] = jnp.zeros((group * rows - 1312, 128), low)
-
-    span = n_line * rows
-
-    def plane_peer(step):
-        index = lax.rem(mine + step, n_plane)
-        return index, (index // 2 * 2 + core, line * 2 + lax.rem(index, 2))
-
-    def line_peer(step):
-        index = lax.rem(line + step, n_line)
-        return index, (tm, index * 2 + lax.rem(pix, 2))
-
-    def span_of(step):
-        index, _ = plane_peer(step)
-        return pl.ds(pl.multiple_of(index * span, 16), span)
-
-    def swap(step):
-        return pltpu.make_async_remote_copy(
-            packed.at[1 - core, span_of(step)], core_in.at[span_of(step)],
-            core_sems.at[0, step], core_sems.at[1, step], partner, MESH
-        )
-
-    def to_plane(step):
-        return pltpu.make_async_remote_copy(
-            half.at[span_of(step)], plane_in.at[step],
-            plane_sems.at[0, step], plane_sems.at[1, step], plane_peer(step)[1], MESH
-        )
-
-    def to_line(step):
-        index, device = line_peer(step)
-        return pltpu.make_async_remote_copy(
-            line_out.at[index], line_in.at[step],
-            line_sems.at[0, step], line_sems.at[1, step], device, MESH
-        )
-
-    order = list(range(1, n_plane)) + [0]
-    for step in order:
-        swap(step).start()
-    for step in order:
-        swap(step).wait()
-        at = span_of(step)
-        half[at, :] = (packed[core, at, :].astype(f32) + core_in[at, :].astype(f32)).astype(low)
-        if step:
-            to_plane(step).start()
+        packed[side, size + C + 32 :, :] = jnp.zeros((group * rest_rows - C - 32, 128), low)
+    rest[0]()
+    down[4]()
 
     for child in range(4):
         lanes = slice(child * C, child * C + C)
@@ -324,26 +440,7 @@
         )
         for side in range(2):
             fine[side, pl.ds(child, TR * TC, stride=4), :] = value[:, side * 128 : side * 128 + 128]
-
-    for step in range(1, n_plane):
-        to_plane(step).wait()
-
-    def line_sum(step):
-        index, _ = line_peer(step)
-        at = pl.ds(pl.multiple_of(mine * span + index * rows, 16), rows)
-        total = half[at, :].astype(f32)
-        for other in range(1, n_plane):
-            total = total + plane_in[
-                other, pl.ds(pl.multiple_of(index * rows, 16), rows), :
-            ].astype(f32)
-        line_out[index] = total.astype(low)
-
-    @pl.loop(1, n_line)
-    def _(step):
-        line_sum(step)
-        to_line(step).start()
-
-    line_sum(0)
+    rest[1]()
 
     @pl.loop(0, 2560 // 160)
     def _(i):
@@ -353,75 +450,27 @@
 
     store = pltpu.make_async_copy(result, out_input, out_sems.at[0])
     store.start()
-
-    @pl.loop(1, n_line)
-    def _(step):
-        to_line(step).wait()
-
-    def add(step, total):
-        return total + line_in[step].astype(f32)
-
-    def place(plane_step, line_step):
-        index = lax.rem(mine + n_plane - plane_step, n_plane) * n_line + lax.rem(
-            line + n_line - line_step, n_line
-        )
-        return full.at[core, pl.ds(pl.multiple_of(index * rows, 16), rows)]
-
-    first = pl.ds(pl.multiple_of((mine * n_line + line) * rows, 16), rows)
-    full[core, first, :] = lax.fori_loop(1, n_line, add, line_out[line].astype(f32)).astype(low)
-
-    def back_line(step):
-        return pltpu.make_async_remote_copy(
-            place(0, 0), place(0, 0),
-            line_back.at[0, step], line_back.at[1, step], line_peer(step)[1], MESH
-        )
-
-    def back_plane(plane_step, step):
-        return pltpu.make_async_remote_copy(
-            place(0, step), place(0, step), plane_send.at[plane_step, step],
-            plane_recv.at[plane_step, step], plane_peer(plane_step)[1], MESH
-        )
-
-    def back_pair(plane_step, step):
-        return pltpu.make_async_remote_copy(
-            place(plane_step, step), place(plane_step, step), pair_send.at[plane_step, step],
-            pair_recv.at[plane_step, step], partner, MESH
-        )
-
-    @pl.loop(1, n_line)
-    def _(step):
-        back_line(step).start()
-
-    for plane_step in range(1, n_plane):
-        back_plane(plane_step, 0).start()
-    back_pair(0, 0).start()
-
-    @pl.loop(1, n_line)
-    def _(step):
-        back_line(step).wait()
-        for plane_step in range(1, n_plane):
-            back_plane(plane_step, step).start()
-        back_pair(0, step).start()
-
-    @pl.loop(0, n_line)
-    def _(step):
-        for plane_step in range(1, n_plane):
-            back_plane(plane_step, step).wait()
-            back_pair(plane_step, step).start()
-
-    @pl.loop(0, n_line)
-    def _(step):
-        for plane_step in range(n_plane):
-            back_pair(plane_step, step).wait()
-
-    store_full = pltpu.make_async_copy(full, out_full, out_sems.at[1])
-    store_full.start()
+    rest[2]()
+    down[5]()
+    rest[3]()
+    down[6]()
+    store_down = pltpu.make_async_copy(
+        full.at[:, 0:size], out_full.at[:, 0:size], out_sems.at[1]
+    )
+    store_down.start()
+    for stage in rest[4:]:
+        stage()
+    store_rest = pltpu.make_async_copy(
+        full.at[:, size:], out_full.at[:, size:], out_sems.at[2]
+    )
+    store_rest.start()
     store.wait()
-    store_full.wait()
+    store_down.wait()
+    store_rest.wait()
 
 
 def unpack_kernel(
-    scale, fine_in, full_in, out_input, out_down, out_bias, out_taps, out_point, out_mix,
+    scale, size, fine_in, full_in, out_input, out_down, out_bias, out_taps, out_point, out_mix,
     full, down, bias, taps, point, mix, sems,
 ):
     f32 = jnp.float32
@@ -432,13 +481,13 @@
     load.wait()
     for side in range(2):
         lanes = slice(side * 128, side * 128 + 128)
-        tail = full[side, 5 * C : 5 * C + 32, :].astype(f32) * scale
+        tail = full[side, size + C : size + C + 32, :].astype(f32) * scale
         taps[:, lanes] = tail[0:9]
         for frame in range(mix.shape[0]):
             first = 9 + frame * mix.shape[1]
             mix[frame, :, lanes] = tail[first : first + mix.shape[1]]
         bias[lanes] = tail[25]
-        point[:, lanes] = full[side, 4 * C : 5 * C, :].astype(f32) * scale
+        point[:, lanes] = full[side, size : size + C, :].astype(f32) * scale
         down[:, lanes] = full[side, 0 : 4 * C, :].astype(f32) * scale
     stores = [
         pltpu.make_async_copy(here, there, sems.at[2 + i])
@@ -462,17 +511,19 @@
     quarter = pixels // frames
     scale = 1.0 / math.sqrt(frames * tiles * pixels)
     group = frames // 2 * tiles
-    rows = -(-1312 // (16 * group)) * 16
+    rows = -(-4 * C // (16 * group)) * 16
+    rest_rows = -(-(C + 32) // (16 * group)) * 16
+    size = group * (rows + rest_rows)
     f32, low = jnp.float32, jnp.bfloat16
     both = lambda n: pltpu.SemaphoreType.DMA((2, n))
     n_plane, n_line = frames // 2 * 2, tiles // 2
     grid = pltpu.SemaphoreType.DMA((n_plane, n_line))
     hbm = pl.BlockSpec(memory_space=pltpu.HBM)
     fine, full = pl.pallas_call(
-        functools.partial(kernel, rows),
+        functools.partial(kernel, rows, rest_rows),
         out_shape=[
             jax.ShapeDtypeStruct((4 * pixels, C), low),
-            jax.ShapeDtypeStruct((2, group * rows, 128), low),
+            jax.ShapeDtypeStruct((2, size, 128), low),
         ],
         in_specs=[hbm] * 8,
         out_specs=[hbm] * 2,
@@ -507,20 +558,23 @@
             pltpu.VMEM((2, 32, C), low),
             pltpu.VMEM((2, 32, C), low),
             pltpu.VMEM((pixels, C), low),
-            pltpu.VMEM((2, group * rows, 128), low),
-            pltpu.VMEM((group * rows, 128), low),
-            pltpu.VMEM((group * rows, 128), low),
+            pltpu.VMEM((2, size, 128), low),
+            pltpu.VMEM((size, 128), low),
+            pltpu.VMEM((size, 128), low),
+            pltpu.VMEM((2, size, 128), low),
             pltpu.VMEM((n_plane, n_line * rows, 128), low),
             pltpu.VMEM((n_line, rows, 128), low),
             pltpu.VMEM((n_line, rows, 128), low),
-            pltpu.VMEM((2, group * rows, 128), low),
+            pltpu.VMEM((n_plane, n_line * rest_rows, 128), low),
+            pltpu.VMEM((n_line, rest_rows, 128), low),
+            pltpu.VMEM((n_line, rest_rows, 128), low),
             pltpu.SemaphoreType.DMA((8,)),
-            pltpu.SemaphoreType.DMA((2,)),
+            pltpu.SemaphoreType.DMA((3,)),
             both(frames), both(frames), both(2), both(2),
-            both(n_plane), both(n_plane), both(n_line), both(n_line), grid, grid, grid, grid,
-        ],
+        ]
+        + 2 * [both(n_plane), both(n_plane), both(n_line), both(n_line), grid, grid, grid, grid],
         compiler_params=pltpu.CompilerParams(
-            collective_id=0, has_side_effects=True, vmem_limit_bytes=48 * 1024 * 1024
+            collective_id=0, has_side_effects=True, vmem_limit_bytes=64 * 1024 * 1024
         ),
     )(
         activations.reshape(4 * pixels, C),
@@ -534,15 +588,15 @@
     )
     shapes = [(4 * C, C), (C,), (9, C), (C, C), (frames, frames, C)]
     outs = pl.pallas_call(
-        functools.partial(unpack_kernel, scale),
+        functools.partial(unpack_kernel, scale, group * rows),
         out_shape=[jax.ShapeDtypeStruct((4 * pixels, C), low)]
         + [jax.ShapeDtypeStruct(shape, f32) for shape in shapes],
         in_specs=[hbm] * 2,
         out_specs=[hbm] * 6,
-        scratch_shapes=[pltpu.VMEM((2, group * rows, 128), low)]
+        scratch_shapes=[pltpu.VMEM((2, size, 128), low)]
         + [pltpu.VMEM(shape, f32) for shape in shapes]
         + [pltpu.SemaphoreType.DMA((7,))],
-        compiler_params=pltpu.CompilerParams(vmem_limit_bytes=32 * 1024 * 1024),
+        compiler_params=pltpu.CompilerParams(vmem_limit_bytes=64 * 1024 * 1024),
     )(fine, full)
     return (outs[0].reshape(1, 4 * pixels, C), *outs[1:])
 

time: 53.1 us -> 91 us (1.71)
  Pallas kernels: 45 us -> 90.2 us
  local copies, waits for them, and re-layouts: 7.02 us -> 0 us
    pallas_call x2, Pallas kernels: 45 us -> 90.2 us  [the longest x1 49.3 us: on_device(): pl.pallas_call(functools.partial(kernel, rows, rest_rows), out_shape=[jax...]
    unnamed x16 -> x0, local copies, waits for them, and re-layouts: 7.02 us -> none
where the time goes in v4:
time: 91 us; the launch traced here: 90.9 us
  Pallas kernels  90.2 us (99%)
    pallas_call x1, Pallas kernels, on_device(): pl.pallas_call(functools.partial(kernel, rows, rest_rows), out_shape=[jax...  49.3 us
    pallas_call x1, Pallas kernels, on_device(): pl.pallas_call(functools.partial(unpack_kernel, scale, group * rows), out...  40.9 us

profile of v4, /device:TPU:0, one launch (start us, length us, event | category | flops | bytes accessed | tf_op | source)
XLA Modules:
  0.0 90.9 jit_solution(2611988623308296294)
XLA Ops:
  0.6 49.3 %shard_map.127 = (bf16[2560,256]{1,0:T(8,128)(2,1)}, bf16[2,1536,128]{2,1,0:T(8,128)(2,1)}) custom-call(bf16[2560,256]{1,0:T(8,128)(2,1)} %bitcast.3, bf16[1024,256]{1,0:T(8,128)(2,1)} %weight_in.1, f32[1,256]{1,0:T(1,128)} %bitcast.4, f32[9,256]{1,0:T(8,128)} %taps_in.1, bf16[256,256]{1,0:T(8,128)(2,1)} %point_in.1, f32[4,4,256]{2,1,0:T(4,128)} %mix_in.1, ...), custom_call_target="tpu_custom_call" | custom-call | tf_op jit(solution)/shard_map/pallas_call | solution.py:522
  50.0 40.9 %shard_map.128 = (bf16[2560,256]{1,0:T(8,128)(2,1)}, f32[1024,256]{1,0:T(8,128)}, f32[256]{0:T(256)}, f32[9,256]{1,0:T(8,128)}, f32[256,256]{1,0:T(8,128)}, /*index=5*/f32[4,4,256]{2,1,0:T(4,128)}) custom-call(bf16[2560,256]{1,0:T(8,128)(2,1)} %get-tuple-element.14.fine_in, bf16[2,1536,128]{2,1,0:T(8,128)(2,1)} %get-tuple-element.15.full_in), custom_call_target="tpu_custom_call" | custom-call | tf_op jit(solution)/shard_map/pallas_call | solution.py:590

commit v5 on v4

--- a/solution.py
+++ b/solution.py
@@ -191,7 +191,7 @@
         grad[pl.ds(pl.multiple_of(r * TC, TC), TC), :] = value
         return carry
 
-    lax.fori_loop(0, TR, inner, 0)
+    lax.fori_loop(0, TR, inner, 0, unroll=2)
     for copy in backward:
         copy.wait()
     edge[...] = back_recv[...].astype(f32)
@@ -208,7 +208,7 @@
         wider = low_grad.astype(f32)
         return total + ((wider[0:8] + wider[8:16]) + (wider[16:24] + wider[24:32]))
 
-    bias_part = lax.fori_loop(0, TR, through, jnp.zeros((8, C), f32))
+    bias_part = lax.fori_loop(0, TR, through, jnp.zeros((8, C), f32), unroll=4)
     for child in range(4):
         lanes = slice(child * C, child * C + C)
         pack(child * C, jnp.dot(rows_t[lanes, :], pre[...], preferred_element_type=f32))
@@ -226,7 +226,7 @@
         return index, (tm, index * 2 + lax.rem(pix, 2))
 
     def total_stages(base, rows, plane_in, line_out, line_in, sems):
-        core_sems, plane_sems, line_sems, line_back, plane_send, plane_recv, pair_send, pair_recv = sems
+        core_sems, plane_sems, line_sems, line_back, plane_back, pair_back = sems
         span = n_line * rows
         order = list(range(1, n_plane)) + [0]
 
@@ -252,28 +252,27 @@
                 line_sems.at[0, step], line_sems.at[1, step], device, MESH
             )
 
-        def place(plane_step, line_step):
-            index = lax.rem(mine + n_plane - plane_step, n_plane) * n_line + lax.rem(
-                line + n_line - line_step, n_line
-            )
-            return full.at[core, pl.ds(pl.multiple_of(base + index * rows, 16), rows)]
+        own = full.at[core, pl.ds(pl.multiple_of(base + (mine * n_line + line) * rows, 16), rows)]
+
+        def place(step):
+            index = lax.rem(mine + n_plane - step, n_plane)
+            return full.at[core, pl.ds(pl.multiple_of(base + index * span, 16), span)]
 
         def back_line(step):
             return pltpu.make_async_remote_copy(
-                place(0, 0), place(0, 0),
-                line_back.at[0, step], line_back.at[1, step], line_peer(step)[1], MESH
+                own, own, line_back.at[0, step], line_back.at[1, step], line_peer(step)[1], MESH
             )
 
-        def back_plane(plane_step, step):
+        def back_plane(step):
             return pltpu.make_async_remote_copy(
-                place(0, step), place(0, step), plane_send.at[plane_step, step],
-                plane_recv.at[plane_step, step], plane_peer(plane_step)[1], MESH
+                place(0), place(0),
+                plane_back.at[0, step], plane_back.at[1, step], plane_peer(step)[1], MESH
             )
 
-        def back_pair(plane_step, step):
+        def back_pair(step):
             return pltpu.make_async_remote_copy(
-                place(plane_step, step), place(plane_step, step), pair_send.at[plane_step, step],
-                pair_recv.at[plane_step, step], partner, MESH
+                place(step), place(step),
+                pair_back.at[0, step], pair_back.at[1, step], partner, MESH
             )
 
         def start():
@@ -328,36 +327,29 @@
             def _(step):
                 back_line(step).start()
 
-            for plane_step in range(1, n_plane):
-                back_plane(plane_step, 0).start()
-            back_pair(0, 0).start()
-
         def leave_line():
             @pl.loop(1, n_line)
             def _(step):
                 back_line(step).wait()
-                for plane_step in range(1, n_plane):
-                    back_plane(plane_step, step).start()
-                back_pair(0, step).start()
+
+            for step in range(1, n_plane):
+                back_plane(step).start()
+            back_pair(0).start()
 
         def leave_plane():
-            @pl.loop(0, n_line)
-            def _(step):
-                for plane_step in range(1, n_plane):
-                    back_plane(plane_step, step).wait()
-                    back_pair(plane_step, step).start()
+            for step in range(1, n_plane):
+                back_plane(step).wait()
+                back_pair(step).start()
 
         def finish():
-            @pl.loop(0, n_line)
-            def _(step):
-                for plane_step in range(n_plane):
-                    back_pair(plane_step, step).wait()
+            for step in range(n_plane):
+                back_pair(step).wait()
 
         return start, enter_plane, enter_line, turn, leave_line, leave_plane, finish
 
-    down = total_stages(0, rows, plane_in, line_out, line_in, total_sems[:8])
+    down = total_stages(0, rows, plane_in, line_out, line_in, total_sems[:6])
     rest = total_stages(
-        size, rest_rows, rest_plane_in, rest_line_out, rest_line_in, total_sems[8:]
+        size, rest_rows, rest_plane_in, rest_line_out, rest_line_in, total_sems[6:]
     )
     down[0]()
 
@@ -471,13 +463,16 @@
 
 def unpack_kernel(
     scale, size, fine_in, full_in, out_input, out_down, out_bias, out_taps, out_point, out_mix,
-    full, down, bias, taps, point, mix, sems,
+    fine, full, down, bias, taps, point, mix, sems,
 ):
     f32 = jnp.float32
-    through = pltpu.make_async_copy(fine_in, out_input, sems.at[0])
+    through = pltpu.make_async_copy(fine_in, fine, sems.at[7])
     through.start()
     load = pltpu.make_async_copy(full_in, full, sems.at[1])
     load.start()
+    through.wait()
+    through = pltpu.make_async_copy(fine, out_input, sems.at[0])
+    through.start()
     load.wait()
     for side in range(2):
         lanes = slice(side * 128, side * 128 + 128)
@@ -517,7 +512,6 @@
     f32, low = jnp.float32, jnp.bfloat16
     both = lambda n: pltpu.SemaphoreType.DMA((2, n))
     n_plane, n_line = frames // 2 * 2, tiles // 2
-    grid = pltpu.SemaphoreType.DMA((n_plane, n_line))
     hbm = pl.BlockSpec(memory_space=pltpu.HBM)
     fine, full = pl.pallas_call(
         functools.partial(kernel, rows, rest_rows),
@@ -572,7 +566,7 @@
             pltpu.SemaphoreType.DMA((3,)),
             both(frames), both(frames), both(2), both(2),
         ]
-        + 2 * [both(n_plane), both(n_plane), both(n_line), both(n_line), grid, grid, grid, grid],
+        + 2 * [both(n_plane), both(n_plane), both(n_line), both(n_line), both(n_plane), both(n_plane)],
         compiler_params=pltpu.CompilerParams(
             collective_id=0, has_side_effects=True, vmem_limit_bytes=64 * 1024 * 1024
         ),
@@ -593,9 +587,9 @@
         + [jax.ShapeDtypeStruct(shape, f32) for shape in shapes],
         in_specs=[hbm] * 2,
         out_specs=[hbm] * 6,
-        scratch_shapes=[pltpu.VMEM((2, size, 128), low)]
+        scratch_shapes=[pltpu.VMEM((4 * pixels, C), low), pltpu.VMEM((2, size, 128), low)]
         + [pltpu.VMEM(shape, f32) for shape in shapes]
-        + [pltpu.SemaphoreType.DMA((7,))],
+        + [pltpu.SemaphoreType.DMA((8,))],
         compiler_params=pltpu.CompilerParams(vmem_limit_bytes=64 * 1024 * 1024),
     )(fine, full)
     return (outs[0].reshape(1, 4 * pixels, C), *outs[1:])

time: 91 us -> 52.4 us (0.58)
  Pallas kernels: 90.2 us -> 51.6 us
    pallas_call x1, Pallas kernels: 40.9 us -> 2.88 us  [on_device(): pl.pallas_call(functools.partial(unpack_kernel, scale, group * rows), out...]
where the time goes in v5:
time: 52.4 us; the launch traced here: 52.2 us
  Pallas kernels  51.6 us (98%)
  between operations  0.64 us (1%)
    pallas_call x1, Pallas kernels, on_device(): pl.pallas_call(functools.partial(kernel, rows, rest_rows), out_shape=[jax...  48.7 us
    pallas_call x1, Pallas kernels, on_device(): pl.pallas_call(functools.partial(unpack_kernel, scale, group * rows), out...  2.88 us

profile of v5, /device:TPU:0, one launch (start us, length us, event | category | flops | bytes accessed | tf_op | source)
XLA Modules:
  0.0 52.2 jit_solution(14808452448057221605)
XLA Ops:
  0.6 48.7 %shard_map.127 = (bf16[2560,256]{1,0:T(8,128)(2,1)}, bf16[2,1536,128]{2,1,0:T(8,128)(2,1)}) custom-call(bf16[2560,256]{1,0:T(8,128)(2,1)} %bitcast.3, bf16[1024,256]{1,0:T(8,128)(2,1)} %weight_in.1, f32[1,256]{1,0:T(1,128)} %bitcast.4, f32[9,256]{1,0:T(8,128)} %taps_in.1, bf16[256,256]{1,0:T(8,128)(2,1)} %point_in.1, f32[4,4,256]{2,1,0:T(4,128)} %mix_in.1, ...), custom_call_target="tpu_custom_call" | custom-call | tf_op jit(solution)/shard_map/pallas_call | solution.py:516
  49.3 2.9 %shard_map.128 = (bf16[2560,256]{1,0:T(8,128)(2,1)}, f32[1024,256]{1,0:T(8,128)}, f32[256]{0:T(256)}, f32[9,256]{1,0:T(8,128)}, f32[256,256]{1,0:T(8,128)}, /*index=5*/f32[4,4,256]{2,1,0:T(4,128)}) custom-call(bf16[2560,256]{1,0:T(8,128)(2,1)} %get-tuple-element.14.fine_in, bf16[2,1536,128]{2,1,0:T(8,128)(2,1)} %get-tuple-element.15.full_in), custom_call_target="tpu_custom_call" | custom-call | tf_op jit(solution)/shard_map/pallas_call | solution.py:584

commit v6 on v3

--- a/solution.py
+++ b/solution.py
@@ -22,7 +22,7 @@
     mg_send, mg_recv, mix_send, mix_recv, edge, edge_send, edge_recv, back_send, back_recv, pre,
     packed, core_in, half, plane_in, line_out, line_in, full,
     in_sems, out_sems, mg_sems, mix_sems, edge_sems, back_sems,
-    core_sems, plane_sems, line_sems, line_back, plane_send, plane_recv, pair_send, pair_recv,
+    core_sems, plane_sems, line_sems, line_back, plane_back, pair_back,
 ):
     f32, low = jnp.float32, jnp.bfloat16
     tm, pix = lax.axis_index("tm"), lax.axis_index("pix")
@@ -245,10 +245,24 @@
         wider = low_grad.astype(f32)
         return total + ((wider[0:8] + wider[8:16]) + (wider[16:24] + wider[24:32]))
 
-    bias_part = lax.fori_loop(0, TR, through, jnp.zeros((8, C), f32))
+    span = n_line * rows
+
+    def swap(block):
+        at = pl.ds(pl.multiple_of(block * span, 16), span)
+        return pltpu.make_async_remote_copy(
+            packed.at[1 - core, at], core_in.at[at],
+            core_sems.at[0, block], core_sems.at[1, block], partner, MESH
+        )
+
+    started = 0
+    bias_part = lax.fori_loop(0, TR, through, jnp.zeros((8, C), f32), unroll=4)
     for child in range(4):
         lanes = slice(child * C, child * C + C)
         pack(child * C, jnp.dot(rows_t[lanes, :], pre[...], preferred_element_type=f32))
+        ready = (child + 1) * C if child < 3 else 5 * C
+        while started < n_plane and (started + 1) * span <= ready:
+            swap(started).start()
+            started += 1
 
     for step in range(1, n_tm):
         exchange(mix_send, mix_recv, mix_sems, step).wait()
@@ -274,8 +288,6 @@
     for side in range(2):
         packed[side, 1312:, :] = jnp.zeros((group * rows - 1312, 128), low)
 
-    span = n_line * rows
-
     def plane_peer(step):
         index = lax.rem(mine + step, n_plane)
         return index, (index // 2 * 2 + core, line * 2 + lax.rem(index, 2))
@@ -288,12 +300,6 @@
         index, _ = plane_peer(step)
         return pl.ds(pl.multiple_of(index * span, 16), span)
 
-    def swap(step):
-        return pltpu.make_async_remote_copy(
-            packed.at[1 - core, span_of(step)], core_in.at[span_of(step)],
-            core_sems.at[0, step], core_sems.at[1, step], partner, MESH
-        )
-
     def to_plane(step):
         return pltpu.make_async_remote_copy(
             half.at[span_of(step)], plane_in.at[step],
@@ -308,10 +314,10 @@
         )
 
     order = list(range(1, n_plane)) + [0]
+    for block in range(started, n_plane):
+        swap(block).start()
     for step in order:
-        swap(step).start()
-    for step in order:
-        swap(step).wait()
+        swap(plane_peer(step)[0]).wait()
         at = span_of(step)
         half[at, :] = (packed[core, at, :].astype(f32) + core_in[at, :].astype(f32)).astype(low)
         if step:
@@ -361,58 +367,48 @@
     def add(step, total):
         return total + line_in[step].astype(f32)
 
-    def place(plane_step, line_step):
-        index = lax.rem(mine + n_plane - plane_step, n_plane) * n_line + lax.rem(
-            line + n_line - line_step, n_line
-        )
-        return full.at[core, pl.ds(pl.multiple_of(index * rows, 16), rows)]
-
     first = pl.ds(pl.multiple_of((mine * n_line + line) * rows, 16), rows)
     full[core, first, :] = lax.fori_loop(1, n_line, add, line_out[line].astype(f32)).astype(low)
 
+    own = full.at[core, first]
+
+    def place(step):
+        index = lax.rem(mine + n_plane - step, n_plane)
+        return full.at[core, pl.ds(pl.multiple_of(index * span, 16), span)]
+
     def back_line(step):
         return pltpu.make_async_remote_copy(
-            place(0, 0), place(0, 0),
-            line_back.at[0, step], line_back.at[1, step], line_peer(step)[1], MESH
-        )
-
-    def back_plane(plane_step, step):
-        return pltpu.make_async_remote_copy(
-            place(0, step), place(0, step), plane_send.at[plane_step, step],
-            plane_recv.at[plane_step, step], plane_peer(plane_step)[1], MESH
-        )
-
-    def back_pair(plane_step, step):
-        return pltpu.make_async_remote_copy(
-            place(plane_step, step), place(plane_step, step), pair_send.at[plane_step, step],
-            pair_recv.at[plane_step, step], partner, MESH
+            own, own, line_back.at[0, step], line_back.at[1, step], line_peer(step)[1], MESH
+        )
+
+    def back_plane(step):
+        return pltpu.make_async_remote_copy(
+            place(0), place(0),
+            plane_back.at[0, step], plane_back.at[1, step], plane_peer(step)[1], MESH
+        )
+
+    def back_pair(step):
+        return pltpu.make_async_remote_copy(
+            place(step), place(step),
+            pair_back.at[0, step], pair_back.at[1, step], partner, MESH
         )
 
     @pl.loop(1, n_line)
     def _(step):
         back_line(step).start()
 
-    for plane_step in range(1, n_plane):
-        back_plane(plane_step, 0).start()
-    back_pair(0, 0).start()
-
     @pl.loop(1, n_line)
     def _(step):
         back_line(step).wait()
-        for plane_step in range(1, n_plane):
-            back_plane(plane_step, step).start()
-        back_pair(0, step).start()
-
-    @pl.loop(0, n_line)
-    def _(step):
-        for plane_step in range(1, n_plane):
-            back_plane(plane_step, step).wait()
-            back_pair(plane_step, step).start()
-
-    @pl.loop(0, n_line)
-    def _(step):
-        for plane_step in range(n_plane):
-            back_pair(plane_step, step).wait()
+
+    for step in range(1, n_plane):
+        back_plane(step).start()
+    back_pair(0).start()
+    for step in range(1, n_plane):
+        back_plane(step).wait()
+        back_pair(step).start()
+    for step in range(n_plane):
+        back_pair(step).wait()
 
     store_full = pltpu.make_async_copy(full, out_full, out_sems.at[1])
     store_full.start()
@@ -422,13 +418,16 @@
 
 def unpack_kernel(
     scale, fine_in, full_in, out_input, out_down, out_bias, out_taps, out_point, out_mix,
-    full, down, bias, taps, point, mix, sems,
+    fine, full, down, bias, taps, point, mix, sems,
 ):
     f32 = jnp.float32
-    through = pltpu.make_async_copy(fine_in, out_input, sems.at[0])
+    through = pltpu.make_async_copy(fine_in, fine, sems.at[7])
     through.start()
     load = pltpu.make_async_copy(full_in, full, sems.at[1])
     load.start()
+    through.wait()
+    through = pltpu.make_async_copy(fine, out_input, sems.at[0])
+    through.start()
     load.wait()
     for side in range(2):
         lanes = slice(side * 128, side * 128 + 128)
@@ -466,7 +465,6 @@
     f32, low = jnp.float32, jnp.bfloat16
     both = lambda n: pltpu.SemaphoreType.DMA((2, n))
     n_plane, n_line = frames // 2 * 2, tiles // 2
-    grid = pltpu.SemaphoreType.DMA((n_plane, n_line))
     hbm = pl.BlockSpec(memory_space=pltpu.HBM)
     fine, full = pl.pallas_call(
         functools.partial(kernel, rows),
@@ -517,10 +515,10 @@
             pltpu.SemaphoreType.DMA((8,)),
             pltpu.SemaphoreType.DMA((2,)),
             both(frames), both(frames), both(2), both(2),
-            both(n_plane), both(n_plane), both(n_line), both(n_line), grid, grid, grid, grid,
+            both(n_plane), both(n_plane), both(n_line), both(n_line), both(n_plane), both(n_plane),
         ],
         compiler_params=pltpu.CompilerParams(
-            collective_id=0, has_side_effects=True, vmem_limit_bytes=48 * 1024 * 1024
+            collective_id=0, has_side_effects=True, vmem_limit_bytes=64 * 1024 * 1024
         ),
     )(
         activations.reshape(4 * pixels, C),
@@ -539,10 +537,10 @@
         + [jax.ShapeDtypeStruct(shape, f32) for shape in shapes],
         in_specs=[hbm] * 2,
         out_specs=[hbm] * 6,
-        scratch_shapes=[pltpu.VMEM((2, group * rows, 128), low)]
+        scratch_shapes=[pltpu.VMEM((4 * pixels, C), low), pltpu.VMEM((2, group * rows, 128), low)]
         + [pltpu.VMEM(shape, f32) for shape in shapes]
-        + [pltpu.SemaphoreType.DMA((7,))],
-        compiler_params=pltpu.CompilerParams(vmem_limit_bytes=32 * 1024 * 1024),
+        + [pltpu.SemaphoreType.DMA((8,))],
+        compiler_params=pltpu.CompilerParams(vmem_limit_bytes=64 * 1024 * 1024),
     )(fine, full)
     return (outs[0].reshape(1, 4 * pixels, C), *outs[1:])
 

time: 53.1 us -> 47.3 us (0.89)
  local copies, waits for them, and re-layouts: 7.02 us -> 0 us
  Pallas kernels: 45 us -> 46.5 us
    unnamed x16 -> x0, local copies, waits for them, and re-layouts: 7.02 us -> none
    pallas_call x1, Pallas kernels: 1.56 us -> 2.88 us  [on_device(): pl.pallas_call(functools.partial(unpack_kernel, scale), out_shape=[jax.Sh...]
where the time goes in v6:
time: 47.3 us; the launch traced here: 47.1 us
  Pallas kernels  46.5 us (98%)
  between operations  0.64 us (1%)
    pallas_call x1, Pallas kernels, on_device(): pl.pallas_call(functools.partial(kernel, rows), out_shape=[jax.ShapeDtype...  43.6 us
    pallas_call x1, Pallas kernels, on_device(): pl.pallas_call(functools.partial(unpack_kernel, scale), out_shape=[jax.Sh...  2.88 us

profile of v6, /device:TPU:0, one launch (start us, length us, event | category | flops | bytes accessed | tf_op | source)
XLA Modules:
  0.0 47.1 jit_solution(4331615499715142212)
XLA Ops:
  0.6 43.6 %shard_map.127 = (bf16[2560,256]{1,0:T(8,128)(2,1)}, bf16[2,1536,128]{2,1,0:T(8,128)(2,1)}) custom-call(bf16[2560,256]{1,0:T(8,128)(2,1)} %bitcast.3, bf16[1024,256]{1,0:T(8,128)(2,1)} %weight_in.1, f32[1,256]{1,0:T(1,128)} %bitcast.4, f32[9,256]{1,0:T(8,128)} %taps_in.1, bf16[256,256]{1,0:T(8,128)(2,1)} %point_in.1, f32[4,4,256]{2,1,0:T(4,128)} %mix_in.1, ...), custom_call_target="tpu_custom_call" | custom-call | tf_op jit(solution)/shard_map/pallas_call | solution.py:469
  44.2 2.9 %shard_map.128 = (bf16[2560,256]{1,0:T(8,128)(2,1)}, f32[1024,256]{1,0:T(8,128)}, f32[256]{0:T(256)}, f32[9,256]{1,0:T(8,128)}, f32[256,256]{1,0:T(8,128)}, /*index=5*/f32[4,4,256]{2,1,0:T(4,128)}) custom-call(bf16[2560,256]{1,0:T(8,128)(2,1)} %get-tuple-element.14.fine_in, bf16[2,1536,128]{2,1,0:T(8,128)(2,1)} %get-tuple-element.15.full_in), custom_call_target="tpu_custom_call" | custom-call | tf_op jit(solution)/shard_map/pallas_call | solution.py:534

commit v7 on v6

--- a/solution.py
+++ b/solution.py
@@ -88,7 +88,7 @@
         row = lax.broadcasted_iota(jnp.int32, (TR, TR), 0)
         perm[side, 0:TR, 0:TR] = jnp.where(maps[0, side : side + 1, :] == row, 1.0, 0.0)
 
-    @pl.loop(0, 2560 // 160)
+    @pl.loop(0, 2560 // 160, unroll=4)
     def _(i):
         at = pl.ds(pl.multiple_of(i * 160, 160), 160)
         for side in range(2):
@@ -206,7 +206,7 @@
         grad[at, :] = inner
         return tuple(new)
 
-    sums = lax.fori_loop(0, TR, conv, tuple(jnp.zeros((8, C), f32) for _ in range(9)))
+    sums = lax.fori_loop(0, TR, conv, tuple(jnp.zeros((8, C), f32) for _ in range(9)), unroll=2)
     taps_part = [jnp.sum(x, axis=0, keepdims=True) for x in sums]
 
     @pl.loop(0, n_tm)
@@ -351,7 +351,7 @@
 
     line_sum(0)
 
-    @pl.loop(0, 2560 // 160)
+    @pl.loop(0, 2560 // 160, unroll=4)
     def _(i):
         at = pl.ds(pl.multiple_of(i * 160, 160), 160)
         for side in range(2):

time: 47.3 us -> 47.1 us (level)
  no operation moved by 1% of the time
where the time goes in v7:
time: 47.1 us; the launch traced here: 47 us
  Pallas kernels  46.3 us (98%)
  between operations  0.64 us (1%)
    pallas_call x1, Pallas kernels, on_device(): pl.pallas_call(functools.partial(kernel, rows), out_shape=[jax.ShapeDtype...  43.4 us
    pallas_call x1, Pallas kernels, on_device(): pl.pallas_call(functools.partial(unpack_kernel, scale), out_shape=[jax.Sh...  2.88 us

profile of v7, /device:TPU:0, one launch (start us, length us, event | category | flops | bytes accessed | tf_op | source)
XLA Modules:
  0.0 47.0 jit_solution(5983912104086431940)
XLA Ops:
  0.6 43.4 %shard_map.127 = (bf16[2560,256]{1,0:T(8,128)(2,1)}, bf16[2,1536,128]{2,1,0:T(8,128)(2,1)}) custom-call(bf16[2560,256]{1,0:T(8,128)(2,1)} %bitcast.3, bf16[1024,256]{1,0:T(8,128)(2,1)} %weight_in.1, f32[1,256]{1,0:T(1,128)} %bitcast.4, f32[9,256]{1,0:T(8,128)} %taps_in.1, bf16[256,256]{1,0:T(8,128)(2,1)} %point_in.1, f32[4,4,256]{2,1,0:T(4,128)} %mix_in.1, ...), custom_call_target="tpu_custom_call" | custom-call | tf_op jit(solution)/shard_map/pallas_call | solution.py:469
  44.1 2.9 %shard_map.128 = (bf16[2560,256]{1,0:T(8,128)(2,1)}, f32[1024,256]{1,0:T(8,128)}, f32[256]{0:T(256)}, f32[9,256]{1,0:T(8,128)}, f32[256,256]{1,0:T(8,128)}, /*index=5*/f32[4,4,256]{2,1,0:T(4,128)}) custom-call(bf16[2560,256]{1,0:T(8,128)(2,1)} %get-tuple-element.14.fine_in, bf16[2,1536,128]{2,1,0:T(8,128)(2,1)} %get-tuple-element.15.full_in), custom_call_target="tpu_custom_call" | custom-call | tf_op jit(solution)/shard_map/pallas_call | solution.py:534
